TPU v7x, 128 devices: a whole 4x4x4 slice. The times are simulated.
128 devices in a mesh: tile: 32 (over x, z, core), chan: 4 (over y).
Axes of the slice: x: 4, y: 4, z: 4, core: 2. Of those that a mesh axis runs over, the one named last changes fastest.
Arguments:
- visibilities: float32 [4, 8192, 128], P('chan', 'tile'), may hold values from -6 to 6
- kernels: bfloat16 [4, 32, 2, 64, 128], P('chan'), may hold values from -0.75 to 0.75
- destination: int32 [4, 8192, 1], P('chan', 'tile'), may hold values from 0 to 31; in each aligned block of 256 rows (0 to 255, 256 to 511, ..., all dimensions but the last counted through in order) at most 24 rows name the same one
- cell: int32 [4, 8192], P('chan', 'tile'), may hold values from 0 to 511
- plane: int32 [4, 8192], P('chan', 'tile'), may hold values from 0 to 31
Outputs:
- image: float32 [1024, 1024], P('chan', 'tile')
Inputs may be any that keep to these rules, and one draw needn't show every extreme that they name: `destination`: in the rows of one device (aligned blocks of 256 rows), no tile is named more than 24 times; some tile is named exactly 24 times in some devices' rows.
All inputs are finite; a program needn't handle non-finite values.
Results may differ from a plain program's by a relative error of at most 0.0059.
Values may be sent and summed in bfloat16 or wider, within the bound.
A program may use at most 320 MiB of HBM per device.

v0:
```python
import math

import jax
import jax.numpy as jnp
from jax import lax
from jax.sharding import PartitionSpec as P

G = 8192
S = 64
NW = 32
P_SIZE = 1024


def phase_tables(row_count, grid_width, pixels):
    spacing = grid_width // pixels - 1
    row_index = jnp.arange(row_count, dtype=jnp.int32)
    pixel_index = jnp.arange(pixels, dtype=jnp.int32)
    product = jnp.mod(
        (row_index[:, None] - grid_width // 2) * (spacing * (pixel_index[None, :] - pixels // 2)),
        grid_width,
    )
    phase_angle = product.astype(jnp.float32) * (2.0 * math.pi / grid_width)
    return (jnp.cos(phase_angle).astype(jnp.bfloat16), jnp.sin(phase_angle).astype(jnp.bfloat16))


def block_patches(samples, kernel_rows):
    sample_count = samples.shape[1] // 2
    support = kernel_rows.shape[3] // 2
    vis_real = samples[:, :sample_count, None]
    vis_imag = samples[:, sample_count:, None]
    kern_real = kernel_rows[:, 0, :, support:].astype(jnp.float32)
    kern_imag = kernel_rows[:, 1, :, support:].astype(jnp.float32)
    weighted_real = (vis_real * kern_real - vis_imag * kern_imag).astype(jnp.bfloat16)
    weighted_imag = (vis_real * kern_imag + vis_imag * kern_real).astype(jnp.bfloat16)
    u_kernel = kernel_rows[:, :, :, :support]
    v_weighted = jnp.stack(
        [
            jnp.stack([weighted_real, weighted_imag], 2),
            jnp.stack([-weighted_imag, weighted_real], 2),
        ],
        1,
    )
    return jnp.einsum("bpkx,bpkqy->bxqy", u_kernel, v_weighted, preferred_element_type=jnp.float32)


def local(visibilities, kernels, destination, cell, plane):
    tile_count = lax.axis_size("tile")
    tile_index = lax.axis_index("tile")
    samples = visibilities[0]
    kernel_set = kernels[0]
    owners = destination[0, :, 0]
    blocks = samples.shape[0]
    capacity = 3 * blocks // tile_count
    onehot = (owners[:, None] == jnp.arange(tile_count, dtype=jnp.int32)[None, :]).astype(jnp.int32)
    slot_rank = jnp.sum(jnp.cumsum(onehot, axis=0) * onehot, axis=1) - 1
    packed_meta = cell[0] * NW + plane[0]
    send_samples = (
        jnp.zeros((tile_count, capacity, samples.shape[1]), jnp.float32)
        .at[owners, slot_rank]
        .set(samples)
    )
    send_meta = jnp.zeros((tile_count, capacity), jnp.int32).at[owners, slot_rank].set(packed_meta)
    arrived, arrived_meta = (
        lax.all_to_all(send_samples, "tile", split_axis=0, concat_axis=0, tiled=True),
        lax.all_to_all(send_meta, "tile", split_axis=0, concat_axis=0, tiled=True),
    )
    slot_total = tile_count * capacity
    stride = math.gcd(slot_total, 256)
    arrived = arrived.reshape(slot_total // stride, stride, samples.shape[1])
    arrived_meta = arrived_meta.reshape(slot_total // stride, stride)
    slab_rows = G // tile_count
    cell_cols = G // S

    def add_block(grid_cells, blk):
        sample_blk, meta_blk = blk
        patches = block_patches(sample_blk, kernel_set[meta_blk % NW])
        return (grid_cells.at[meta_blk // NW].add(patches), None)

    grid_start = jnp.zeros((slab_rows // S * cell_cols, S, 2, S), jnp.float32)
    grid_cells, _ = lax.scan(add_block, grid_start, (arrived, arrived_meta))
    grid_round = grid_cells.astype(jnp.bfloat16).reshape(slab_rows // S, cell_cols, S, 2, S)
    cosine, sine = phase_tables(G, G, P_SIZE)
    with_cosine = jnp.einsum(
        "acxpy,cym->pmax",
        grid_round,
        cosine.reshape(cell_cols, S, P_SIZE),
        preferred_element_type=jnp.float32,
    ).reshape(2, P_SIZE, slab_rows)
    with_sine = jnp.einsum(
        "acxpy,cym->pmax",
        grid_round,
        sine.reshape(cell_cols, S, P_SIZE),
        preferred_element_type=jnp.float32,
    ).reshape(2, P_SIZE, slab_rows)
    transformed = jnp.stack([with_cosine[0] - with_sine[1], with_sine[0] + with_cosine[1]]).astype(
        jnp.bfloat16
    )
    own_cosine = lax.dynamic_slice_in_dim(cosine, tile_index * slab_rows, slab_rows, 0)
    own_sine = lax.dynamic_slice_in_dim(sine, tile_index * slab_rows, slab_rows, 0)
    columns = lax.psum_scatter(
        jnp.dot(transformed[0], own_cosine, preferred_element_type=jnp.float32)
        - jnp.dot(transformed[1], own_sine, preferred_element_type=jnp.float32),
        "tile",
        scatter_dimension=0,
        tiled=True,
    )
    summed = lax.psum_scatter(columns, "chan", scatter_dimension=1, tiled=True)
    return summed.T * (1.0 / G)


def solution(mesh):
    placed = (
        P("chan", "tile", None),
        P("chan", None, None, None, None),
        P("chan", "tile", None),
        P("chan", "tile"),
        P("chan", "tile"),
    )
    return jax.shard_map(
        local, mesh=mesh, in_specs=placed, out_specs=P("chan", "tile"), check_vma=False
    )
```

profile of v0, /device:TPU:1, one launch (start us, length us, event | category | flops | bytes accessed | tf_op | source)
XLA Modules:
  0.0 845.9 jit_solution(3143902207157288593)
XLA Ops:
  10.2 12.7 %scatter_fusion.1 = s32[32,24]{0,1:T(8,128)S(1)} fusion(s32[32,24]{0,1:T(8,128)S(1)} %broadcast_in_dim.7, s32[256]{0:T(256)S(1)} %bitcast.143, s32[256]{0:T(256)S(1)} %bitcast.154), kind=kCustom, calls=%fused_computation.2 | custom fusion | bytes 5120 | tf_op jit(solution)/shard_map/scatter | solution.py:62
  23.6 9.4 %all-to-all-start = ((s32[32,1,24]{2,1,0:T(1,128)}), s32[32,1,24]{2,1,0:T(1,128)S(1)}, u32[]{:S(2)}, u32[]{:S(2)}) async-start(s32[32,1,24]{2,1,0:T(1,128)} %copy.23), calls=%async_computation | async-start | bytes 32768 | tf_op jit(solution)/shard_map/all_to_all | solution.py:65
  33.9 26.6 %scatter_fusion.2 = f32[32,24,128]{2,1,0:T(8,128)} fusion(f32[32,24,128]{2,1,0:T(8,128)} %broadcast_in_dim.8, s32[256]{0:T(256)S(1)} %bitcast.144, f32[256,128]{1,0:T(8,128)} %bitcast.149), kind=kCustom, calls=%fused_computation.3 | custom fusion | bytes 395264 | tf_op jit(solution)/shard_map/scatter | solution.py:60
  60.4 7.3 all-to-all-start.1
  68.0 19.9 %fusion.15 = f32[8192,1024]{1,0:T(8,128)} fusion(s32[1024]{0:T(1024)S(1)} %add_multiply_fusion, s32[8192]{0:T(1024)S(1)} %iota_add_fusion), kind=kLoop, calls=%fused_computation.47 | loop fusion | flops 117440512 | bytes 33591296 | tf_op jit(solution)/shard_map/mul | solution.py:22
  89.8 11.2 %broadcast_in_dim.6 = f32[512,64,2,64]{3,1,2,0:T(8,128)} broadcast(f32[]{:T(128)} %constant.114.clone.1), dimensions={} | broadcast | bytes 16777220 | tf_op jit(solution)/shard_map/broadcast_in_dim | solution.py:79
  101.0 296.1 %while.12 = (s32[]{:T(128)}, f32[512,64,2,64]{3,1,2,0:T(8,128)}, s32[3,256]{1,0:T(4,128)S(1)}, bf16[32,2,64,128]{3,2,1,0:T(8,128)(2,1)S(1)}, f32[3,256,128]{2,1,0:T(8,128)S(1)}, /*index=5*/s32[]{:T(128)}) while((s32[]{:T(128)}, f32[512,64,2,64]{3,1,2,0:T(8,128)}, s32[3,256]{1,0:T(4,128)S(1)}, bf16[32,2,64,128]{3,2,1,0:T(8,128)(2,1)S(1)}, ...), condition=%wide.region_7.8_spmd, body=%wide.region_5.7_spmd.sunk | while | flops 573579520 | bytes 122434688 | solution.py:80
  101.0 8.3 gather_fusion
  109.5 8.8 %fusion.69 = (bf16[256,64,1,64]{3,1,2,0:T(8,128)(2,1)S(1)}, bf16[256,64,1,64]{3,1,2,0:T(8,128)(2,1)S(1)}) fusion(bf16[256,2,64,128]{3,2,1,0:T(8,128)(2,1)} %gather_fusion, f32[256,64]{1,0:T(8,128)S(1)} %get-tuple-element.137, f32[256,64]{1,0:T(8,128)S(1)} %get-tuple-element.138), kind=kLoop, calls=%fused_computation.97.clone.1 | loop fusion | flops 7340032 | bytes 8519680 | tf_op jit(solution)/shard_map/while/body/eval_jaxpr/neg | solution.py:39
  118.3 7.1 fusion.70
  125.5 6.6 maximum_bitcast_fusion.3
  132.1 14.8 %fusion.71 = f32[256,64,2,64]{3,1,2,0:T(8,128)} fusion(bf16[256,1,64,2,64]{4,2,1,3,0:T(8,128)(2,1)} %get-tuple-element.141, bf16[256,1,64,2,64]{4,2,1,3,0:T(8,128)(2,1)} %get-tuple-element.142, bf16[256,2,64,128]{3,2,1,0:T(8,128)(2,1)} %gather_fusion), kind=kOutput, calls=%fused_computation.12.clone.1 | convolution fusion | flops 553648128 | bytes 25165824 | tf_op jit(solution)/shard_map/while/body/eval_jaxpr/bpkx,bpkqy->bxqy/dot_general | solution.py:43
  147.0 52.7 %scatter_fusion = f32[512,64,2,64]{3,1,2,0:T(8,128)} fusion(f32[512,64,2,64]{3,1,2,0:T(8,128)} %get-tuple-element.150, s32[256]{0:T(256)S(1)} %bitcast.150, f32[256,64,2,64]{3,1,2,0:T(8,128)} %fusion.71), kind=kCustom, calls=%fused_computation.1.clone.1 | custom fusion | flops 2097152 | bytes 25166848 | tf_op jit(solution)/shard_map/while/body/eval_jaxpr/scatter-add | solution.py:77
  199.7 8.3 gather_fusion
  208.2 8.8 %fusion.69 = (bf16[256,64,1,64]{3,1,2,0:T(8,128)(2,1)S(1)}, bf16[256,64,1,64]{3,1,2,0:T(8,128)(2,1)S(1)}) fusion(bf16[256,2,64,128]{3,2,1,0:T(8,128)(2,1)} %gather_fusion, f32[256,64]{1,0:T(8,128)S(1)} %get-tuple-element.137, f32[256,64]{1,0:T(8,128)S(1)} %get-tuple-element.138), kind=kLoop, calls=%fused_computation.97.clone.1 | loop fusion | flops 7340032 | bytes 8519680 | tf_op jit(solution)/shard_map/while/body/eval_jaxpr/neg | solution.py:39
  217.0 7.1 fusion.70
  224.2 6.6 maximum_bitcast_fusion.3
  230.8 14.8 %fusion.71 = f32[256,64,2,64]{3,1,2,0:T(8,128)} fusion(bf16[256,1,64,2,64]{4,2,1,3,0:T(8,128)(2,1)} %get-tuple-element.141, bf16[256,1,64,2,64]{4,2,1,3,0:T(8,128)(2,1)} %get-tuple-element.142, bf16[256,2,64,128]{3,2,1,0:T(8,128)(2,1)} %gather_fusion), kind=kOutput, calls=%fused_computation.12.clone.1 | convolution fusion | flops 553648128 | bytes 25165824 | tf_op jit(solution)/shard_map/while/body/eval_jaxpr/bpkx,bpkqy->bxqy/dot_general | solution.py:43
  245.7 52.8 %scatter_fusion = f32[512,64,2,64]{3,1,2,0:T(8,128)} fusion(f32[512,64,2,64]{3,1,2,0:T(8,128)} %get-tuple-element.150, s32[256]{0:T(256)S(1)} %bitcast.150, f32[256,64,2,64]{3,1,2,0:T(8,128)} %fusion.71), kind=kCustom, calls=%fused_computation.1.clone.1 | custom fusion | flops 2097152 | bytes 25166848 | tf_op jit(solution)/shard_map/while/body/eval_jaxpr/scatter-add | solution.py:77
  298.5 8.3 gather_fusion
  306.9 8.8 %fusion.69 = (bf16[256,64,1,64]{3,1,2,0:T(8,128)(2,1)S(1)}, bf16[256,64,1,64]{3,1,2,0:T(8,128)(2,1)S(1)}) fusion(bf16[256,2,64,128]{3,2,1,0:T(8,128)(2,1)} %gather_fusion, f32[256,64]{1,0:T(8,128)S(1)} %get-tuple-element.137, f32[256,64]{1,0:T(8,128)S(1)} %get-tuple-element.138), kind=kLoop, calls=%fused_computation.97.clone.1 | loop fusion | flops 7340032 | bytes 8519680 | tf_op jit(solution)/shard_map/while/body/eval_jaxpr/neg | solution.py:39
  315.8 7.1 fusion.70
  322.9 6.6 maximum_bitcast_fusion.3
  329.6 14.8 %fusion.71 = f32[256,64,2,64]{3,1,2,0:T(8,128)} fusion(bf16[256,1,64,2,64]{4,2,1,3,0:T(8,128)(2,1)} %get-tuple-element.141, bf16[256,1,64,2,64]{4,2,1,3,0:T(8,128)(2,1)} %get-tuple-element.142, bf16[256,2,64,128]{3,2,1,0:T(8,128)(2,1)} %gather_fusion), kind=kOutput, calls=%fused_computation.12.clone.1 | convolution fusion | flops 553648128 | bytes 25165824 | tf_op jit(solution)/shard_map/while/body/eval_jaxpr/bpkx,bpkqy->bxqy/dot_general | solution.py:43
  344.4 52.7 %scatter_fusion = f32[512,64,2,64]{3,1,2,0:T(8,128)} fusion(f32[512,64,2,64]{3,1,2,0:T(8,128)} %get-tuple-element.150, s32[256]{0:T(256)S(1)} %bitcast.150, f32[256,64,2,64]{3,1,2,0:T(8,128)} %fusion.71), kind=kCustom, calls=%fused_computation.1.clone.1 | custom fusion | flops 2097152 | bytes 25166848 | tf_op jit(solution)/shard_map/while/body/eval_jaxpr/scatter-add | solution.py:77
  397.1 18.3 %convert_element_type.143 = bf16[512,64,2,64]{3,1,2,0:T(8,128)(2,1)} convert(f32[512,64,2,64]{3,1,2,0:T(8,128)} %get-tuple-element.73) | non-fusion elementwise | flops 4194304 | bytes 25165824 | tf_op jit(solution)/shard_map/convert_element_type | solution.py:81
  415.4 28.0 %copy.24 = bf16[4,128,64,2,64]{1,2,4,3,0:T(8,128)(2,1)} copy(bf16[4,128,64,2,64]{4,2,3,1,0:T(8,128)(2,1)} %bitcast.145) | data formatting | bytes 16777216 | tf_op jit(solution)/shard_map/reshape | solution.py:81
  443.4 139.9 %fusion.26 = f32[2,1024,4,64]{1,3,0,2:T(8,128)S(1)} fusion(bf16[4,128,64,2,64]{1,2,4,3,0:T(8,128)(2,1)} %copy.24, s32[1024]{0:T(1024)S(1)} %copy-done.3, s32[128,64]{0,1:T(8,128)S(1)} %copy-done.1), kind=kOutput, calls=%fused_computation.57 | convolution fusion | flops 8715763712 | bytes 10522624 | tf_op jit(solution)/shard_map/acxpy,cym->pmax/dot_general | solution.py:89
  583.4 138.7 %fusion.29 = f32[2,1024,4,64]{1,3,0,2:T(8,128)S(1)} fusion(bf16[4,128,64,2,64]{1,2,4,3,0:T(8,128)(2,1)} %copy.24, s32[1024]{0:T(1024)S(1)} %copy-done.3, s32[128,64]{0,1:T(8,128)S(1)} %copy-done.1), kind=kOutput, calls=%fused_computation.58 | convolution fusion | flops 8715763712 | bytes 10522624 | tf_op jit(solution)/shard_map/acxpy,cym->pmax/dot_general | solution.py:83
  728.1 6.6 convolution_subtract_fusion
  734.9 81.3 %reduce-scatter.3.cloned.1.call-done = f32[32,1024]{1,0:T(8,128)} async-done(((f32[1024,1024]{1,0:T(8,128)}), f32[32,1024]{1,0:T(8,128)}) %reduce-scatter.3.cloned.1.call-update) | async-done | bytes 131088 | tf_op jit(solution)/shard_map/reduce_scatter | solution.py:100
  816.1 21.5 %reduce-scatter.5.cloned.1.call-done = f32[32,256]{1,0:T(8,128)} async-done(((f32[32,1024]{1,0:T(8,128)}), f32[32,256]{1,0:T(8,128)}) %reduce-scatter.5.cloned.1.call-update) | async-done | bytes 32784 | tf_op jit(solution)/shard_map/reduce_scatter | solution.py:107
  (65 shorter events, 15.2 us)
Async XLA Ops:
  23.6 36.8 %all-to-all-start = ((s32[32,1,24]{2,1,0:T(1,128)}), s32[32,1,24]{2,1,0:T(1,128)S(1)}, u32[]{:S(2)}, u32[]{:S(2)}) async-start(s32[32,1,24]{2,1,0:T(1,128)} %copy.23), calls=%async_computation | async-start | bytes 32768 | tf_op jit(solution)/shard_map/all_to_all | solution.py:65
  33.1 54.8 %copy-start.2 = (s32[1024]{0:T(1024)}, s32[1024]{0:T(1024)S(1)}, u32[]{:S(2)}) copy-start(s32[1024]{0:T(1024)S(1)} %add_multiply_fusion) | copy-start | bytes 12292
  60.4 29.3 %all-to-all-start.1 = ((f32[32,24,128]{2,1,0:T(8,128)}), f32[32,24,128]{2,1,0:T(8,128)S(1)}, u32[]{:S(2)}, u32[]{:S(2)}) async-start(f32[32,24,128]{2,1,0:T(8,128)} %scatter_fusion.2), calls=%async_computation.1 | async-start | bytes 786432 | tf_op jit(solution)/shard_map/all_to_all | solution.py:64
  67.7 748.4 %reduce-scatter.3.cloned.1.call-start = ((), (), s32[]{:S(2)}) async-start(), calls=%async_computation.4 | async-start | bytes 4325376 | tf_op jit(solution)/shard_map/reduce_scatter | solution.py:100
  89.8 11.3 %copy-start = (bf16[1,32,2,64,128]{4,3,2,1,0:T(8,128)(2,1)S(1)}, bf16[1,32,2,64,128]{4,3,2,1,0:T(8,128)(2,1)}, u32[]{:S(2)}) copy-start(bf16[1,32,2,64,128]{4,3,2,1,0:T(8,128)(2,1)} %param.8) | copy-start | bytes 3145732
  109.3 9.0 %slice-start = ((s8[8388608]{0:T(1024)(128)(4,1)}), s8[4194304]{0:T(1024)(128)(4,1)S(1)}, s32[]{:S(2)}) async-start(s8[8388608]{0:T(1024)(128)(4,1)} %bitcast.139), calls=%async_computation.6 | async-start | bytes 8388608 | tf_op jit(solution)/shard_map/while
  109.5 8.9 %slice-start.1 = ((s8[8388608]{0:T(1024)(128)(4,1)}), s8[4194304]{0:T(1024)(128)(4,1)S(1)}, s32[]{:S(2)}) async-start(s8[8388608]{0:T(1024)(128)(4,1)} %bitcast.139), calls=%async_computation.7 | async-start | bytes 8388608 | tf_op jit(solution)/shard_map/while
  208.0 9.0 %slice-start = ((s8[8388608]{0:T(1024)(128)(4,1)}), s8[4194304]{0:T(1024)(128)(4,1)S(1)}, s32[]{:S(2)}) async-start(s8[8388608]{0:T(1024)(128)(4,1)} %bitcast.139), calls=%async_computation.6 | async-start | bytes 8388608 | tf_op jit(solution)/shard_map/while
  208.1 8.9 %slice-start.1 = ((s8[8388608]{0:T(1024)(128)(4,1)}), s8[4194304]{0:T(1024)(128)(4,1)S(1)}, s32[]{:S(2)}) async-start(s8[8388608]{0:T(1024)(128)(4,1)} %bitcast.139), calls=%async_computation.7 | async-start | bytes 8388608 | tf_op jit(solution)/shard_map/while
  306.8 9.0 %slice-start = ((s8[8388608]{0:T(1024)(128)(4,1)}), s8[4194304]{0:T(1024)(128)(4,1)S(1)}, s32[]{:S(2)}) async-start(s8[8388608]{0:T(1024)(128)(4,1)} %bitcast.139), calls=%async_computation.6 | async-start | bytes 8388608 | tf_op jit(solution)/shard_map/while
  306.9 8.9 %slice-start.1 = ((s8[8388608]{0:T(1024)(128)(4,1)}), s8[4194304]{0:T(1024)(128)(4,1)S(1)}, s32[]{:S(2)}) async-start(s8[8388608]{0:T(1024)(128)(4,1)} %bitcast.139), calls=%async_computation.7 | async-start | bytes 8388608 | tf_op jit(solution)/shard_map/while
  415.4 28.0 %copy-start.1 = (s32[128,64]{0,1:T(8,128)S(1)}, s32[128,64]{0,1:T(8,128)}, u32[]{:S(2)}) copy-start(s32[128,64]{0,1:T(8,128)} %add_add_fusion) | copy-start | bytes 98308
  415.4 28.0 %copy-start.3 = (s32[1024]{0:T(1024)S(1)}, s32[1024]{0:T(1024)}, u32[]{:S(2)}) copy-start(s32[1024]{0:T(1024)} %copy-done.2) | copy-start | bytes 12292
  734.8 102.9 %reduce-scatter.5.cloned.1.call-start = ((), (), s32[]{:S(2)}) async-start(), calls=%async_computation.5 | async-start | bytes 163840 | tf_op jit(solution)/shard_map/reduce_scatter | solution.py:107
Sparse Core Ops, SparseCore 0:
  734.9 81.1 reduce-scatter.2
  818.6 19.0 reduce-scatter.4
where the time goes:
time: 851 us; the launch traced here: 846 us
  matrix products  335 us (39%)
  other arithmetic  271 us (32%)
  local copies, waits for them, and re-layouts  106 us (12%)
  waiting for transfers between devices  103 us (12%)
  starting transfers between devices  17 us (2%)
  between operations  13.5 us (2%)
    scatter-add x3, other arithmetic, add_block(): return (grid_cells.at[meta_blk // NW].add(patches), None)  158 us
    dot_general x1, matrix products, local(): jnp.einsum('acxpy,cym->pmax', grid_round, sine.reshape(cell_cols, S, P_SI...  140 us
    dot_general x1, matrix products, local(): jnp.einsum('acxpy,cym->pmax', grid_round, cosine.reshape(cell_cols, S, P_...  139 us
    reduce_scatter x1, waiting for transfers between devices, local(): lax.psum_scatter(jnp.dot(transformed[0], own_cosine, preferred_element_ty...  81.3 us
    dot_general x3, matrix products, block_patches(): jnp.einsum('bpkx,bpkqy->bxqy', u_kernel, v_weighted, preferred_element_ty...  44.5 us
    reshape x1, local copies, waits for them, and re-layouts, local(): grid_cells.astype(jnp.bfloat16).reshape(slab_rows // S, cell_cols, S, 2, S)  28 us
    scatter x1, local copies, waits for them, and re-layouts, local(): send_samples = jnp.zeros((tile_count, capacity, samples.shape[1]), jnp.fl...  26.6 us
    neg x3, other arithmetic, block_patches(): -weighted_imag  26.5 us
  transfers between devices with their start and end apart: 4, of which 2 were waited for; matrix products, arithmetic and copies ran while one was open for 6% of the time, Pallas kernels for 0%

commit v1 on v0

v1 whole, which is shorter than its diff:
```python
import functools
import math

import jax
import jax.numpy as jnp
import ml_dtypes
import numpy as np
from jax import lax
from jax.experimental import pallas as pl
from jax.experimental.pallas import tpu as pltpu
from jax.sharding import PartitionSpec as P

G = 8192
S = 64
NW = 32
PIX = 1024
NT = 32
NC = 4
BLK = 256
CAP = 31
SLOTS = 32
ALL = NT * SLOTS
MIB = 1 << 20
BF = jnp.bfloat16
F32 = jnp.float32
MESH = pl.DeviceIdType.MESH


def split(table):
    high = table.astype(np.float32).astype(ml_dtypes.bfloat16)
    low = (table - high.astype(np.float64)).astype(ml_dtypes.bfloat16)
    return high, low


def row_tables():
    step = G // PIX - 1
    l0 = np.arange(128)
    angle = 2 * math.pi / 128 * ((step * (l0[:, None] - PIX // 2) * (l0[None, :] - 64)) % 128)
    c, s = np.cos(angle), np.sin(angle)
    over_r = np.block([[c, -s], [s, c]]).astype(np.float32).astype(ml_dtypes.bfloat16)
    pixel = l0[:, None] + 128 * np.arange(8)[None, :]
    angle = 2 * math.pi / G * ((step * (pixel[:, :, None] - PIX // 2) * np.arange(S)) % G)
    c, s = np.cos(angle), np.sin(angle)
    over_x = np.concatenate([np.concatenate([c, -s], 2), np.concatenate([s, c], 2)], 1)
    high, low = split(over_x)
    return over_r, np.concatenate([high, low], 1).reshape(128 * 32, 128)


def column_tables():
    step = G // PIX - 1
    m0 = np.arange(32)
    angle = 2 * math.pi / 32 * ((step * (m0[:, None] - PIX // 2) * (m0[None, :] - 16)) % 32)
    c, s = np.cos(angle), np.sin(angle)
    over_t = np.concatenate(split(np.block([[c, -s], [s, c]])), 0)
    pixel = m0[:, None] + 32 * m0[None, :]
    angle = 2 * math.pi / G * ((step * (pixel[:, :, None] - PIX // 2) * np.arange(256)) % G)
    over_v = np.concatenate([np.cos(angle), -np.sin(angle)], 2) / G
    high, low = split(over_v)
    return over_t, np.concatenate([high, low], 1).reshape(32 * 64, 512)


def iota(shape, axis):
    return lax.broadcasted_iota(jnp.int32, shape, axis)


def dot(a, b):
    return jnp.dot(a, b, preferred_element_type=F32)


def dot_t(a, b):
    return lax.dot_general(a, b, (((1,), (1,)), ((), ())), preferred_element_type=F32)


def fill_slots(samples, dest, cell, plane, skipped):
    column = jnp.bitwise_and(cell, 127)
    owner = lax.shift_right_logical(column, 2)
    inner = jnp.bitwise_and(column, 3)
    row = dest * 4 + lax.shift_right_logical(cell, 7)
    named = iota((NT, BLK), 0) == owner
    one = jnp.where(named, 1.0, 0.0)
    one_b = one.astype(BF)
    before = jnp.where(iota((BLK, BLK), 0) < iota((BLK, BLK), 1), 1.0, 0.0).astype(BF)
    count = dot(one_b, before)
    rank = jnp.sum(one * count, axis=0, keepdims=True).astype(jnp.int32) - skipped
    here = jnp.logical_and(rank >= 0, rank < CAP)
    slot = jnp.where(here, owner * SLOTS + rank, -1)
    pick = jnp.where(iota((ALL, BLK), 0) == slot, 1.0, 0.0).astype(BF)
    lane = iota((128, BLK), 0)
    kind = lax.shift_right_logical(lane, 5)
    value = jnp.where(kind == 0, row, jnp.where(kind == 1, plane, jnp.where(kind == 2, inner, 1)))
    held = jnp.logical_and(here, jnp.logical_or(kind == 3, jnp.bitwise_and(lane, 31) == rank))
    facts = dot_t(one_b, jnp.where(held, value.astype(F32), 0.0).astype(BF))
    last = jnp.where(iota((ALL, NT), 0) == iota((ALL, NT), 1) * SLOTS + CAP, 1.0, 0.0).astype(BF)
    slots = dot(pick, samples.astype(BF)) + dot(last, facts.astype(BF))
    return slots.astype(BF), jnp.sum(one, axis=1, keepdims=True)


def exchange_body(first, samples, dest, cell, plane, skipped, *rest):
    if first:
        kern, recv, table, weight, most, send, send_sem, recv_sem = rest
    else:
        recv, send, send_sem, recv_sem = rest
    me = lax.axis_index("tile")
    chan = lax.axis_index("chan")
    barrier = pltpu.get_barrier_semaphore()

    def greet(i, _):
        pl.semaphore_signal(
            barrier, inc=1, device_id=(lax.rem(me + i, NT), chan), device_id_type=MESH
        )
        return 0

    lax.fori_loop(1, NT, greet, 0)
    slots, named = fill_slots(samples[...], dest[...], cell[...], plane[...], skipped[...])
    send[...] = slots
    pl.semaphore_wait(barrier, NT - 1)

    def copy(i):
        to = lax.rem(me + i, NT)
        return pltpu.make_async_remote_copy(
            src_ref=send.at[pl.ds(pl.multiple_of(to * SLOTS, SLOTS), SLOTS)],
            dst_ref=recv.at[pl.ds(pl.multiple_of(me * SLOTS, SLOTS), SLOTS)],
            send_sem=send_sem.at[i],
            recv_sem=recv_sem.at[i],
            device_id=(to, chan),
            device_id_type=MESH,
        )

    def start(i, _):
        copy(i).start()
        return 0

    lax.fori_loop(1, NT, start, 0)
    own = pl.ds(pl.multiple_of(me * SLOTS, SLOTS), SLOTS)
    recv[own, :] = send[own, :]
    if first:
        most[...] = jnp.broadcast_to(jnp.max(named, axis=0, keepdims=True), (8, 128))
        low = iota((S, 128), 1) < S

        def prepare(w, _):
            both = kern[pl.ds(pl.multiple_of(w * 128, 128), 128), :].astype(F32)
            real, imag = both[:S], both[S:]
            turned = both.T[:S]
            base = pl.multiple_of(w * 128, 128)
            table[pl.ds(base, S), :] = turned
            swapped = pltpu.roll(turned, S, 1)
            table[pl.ds(base + S, S), :] = jnp.where(low, -swapped, swapped)
            weight[pl.ds(base, S), :] = jnp.where(low, pltpu.roll(real, S, 1), imag).astype(BF)
            weight[pl.ds(base + S, S), :] = jnp.where(low, -pltpu.roll(imag, S, 1), real).astype(BF)
            return 0

        lax.fori_loop(0, NW, prepare, 0)

    def wait(i, _):
        copy(i).wait()
        return 0

    lax.fori_loop(1, NT, wait, 0)


def exchange(first, samples, dest, cell, plane, skipped, kern=None):
    vmem = pl.BlockSpec(memory_space=pltpu.VMEM)
    shapes = [jax.ShapeDtypeStruct((ALL, 128), BF)]
    operands = [samples, dest, cell, plane, skipped]
    if first:
        shapes += [
            jax.ShapeDtypeStruct((NW * 128, 128), F32),
            jax.ShapeDtypeStruct((NW * 128, 128), BF),
            jax.ShapeDtypeStruct((8, 128), F32),
        ]
        operands.append(kern)
    return pl.pallas_call(
        functools.partial(exchange_body, first),
        out_shape=shapes,
        in_specs=[vmem] * len(operands),
        out_specs=[vmem] * len(shapes),
        scratch_shapes=[
            pltpu.VMEM((ALL, 128), BF),
            pltpu.SemaphoreType.DMA((NT,)),
            pltpu.SemaphoreType.DMA((NT,)),
        ],
        compiler_params=pltpu.CompilerParams(
            collective_id=0 if first else 2, has_side_effects=True, vmem_limit_bytes=32 * MIB
        ),
        name="exchange" if first else "exchange_more",
    )(*operands)


def grid_body(
    recv, table, weight, over_r, over_x, out, grid, half, fill_a, fill_b, facts_v, facts, sem
):
    lane = iota((ALL, 128), 1)
    slot = iota((ALL, 128), 0)
    blocks = jnp.where(jnp.bitwise_and(slot, SLOTS - 1) == CAP, 0.0, recv[...].astype(F32))
    swapped = pltpu.roll(blocks, S, 1)
    fill_a[...] = jnp.where(lane < S, blocks, swapped)
    fill_b[...] = jnp.where(lane < S, swapped, blocks)
    last = jnp.where(iota((NT, ALL), 1) == iota((NT, ALL), 0) * SLOTS + CAP, 1.0, 0.0).astype(BF)
    raw = dot(last, recv[...])
    code = (pltpu.roll(raw, 64, 1) * 128.0 + raw) * 32.0 + pltpu.roll(raw, 96, 1)
    facts_v[...] = jnp.where(iota((NT, 128), 1) < SLOTS, code, raw).astype(jnp.int32)
    to_scalar = pltpu.make_async_copy(facts_v, facts, sem)
    to_scalar.start()

    def clear(i, _):
        grid[pl.ds(pl.multiple_of(i * 512, 512), 512), :] = jnp.zeros((512, 128), F32)
        return 0

    lax.fori_loop(0, 64, clear, 0)
    to_scalar.wait()

    def from_source(t, _):
        def four(j, _):
            made = []
            for k in range(4):
                i = j * 4 + k
                fact = facts[t, i]
                w = jnp.bitwise_and(fact, 31)
                base = pl.multiple_of(w * 128, 128)
                i = t * SLOTS + i
                left = (
                    fill_a[pl.ds(i, 1), :] * table[pl.ds(base, S), :]
                    + fill_b[pl.ds(i, 1), :] * table[pl.ds(base + S, S), :]
                ).astype(BF)
                patch = dot(left, weight[pl.ds(base, 128), :])
                made.append((lax.shift_right_logical(fact, 5), patch))
            for place, patch in made:
                at = pl.ds(pl.multiple_of(place * S, S), S)
                grid[at, :] = grid[at, :] + patch
            return 0

        lax.fori_loop(0, lax.shift_right_logical(facts[t, 96] + 3, 2), four, 0)
        return 0

    lax.fori_loop(0, NT, from_source, 0)

    def over_rows(x, _):
        part = [grid[pl.ds(i * 8192 + x, 128, stride=S), :] for i in range(4)]
        real = jnp.concatenate([p[:, :S] for p in part], axis=1)
        imag = jnp.concatenate([p[:, S:] for p in part], axis=1)
        got = dot(over_r[...], jnp.concatenate([real, imag], axis=0).astype(BF))
        half[pl.ds(x, 128, stride=128), :] = got[:128, :128]
        half[pl.ds(S + x, 128, stride=128), :] = got[128:, :128]
        half[pl.ds(16384 + x, 128, stride=128), :] = got[:128, 128:]
        half[pl.ds(16384 + S + x, 128, stride=128), :] = got[128:, 128:]
        return 0

    lax.fori_loop(0, S, over_rows, 0)
    pixels = grid

    def over_offsets(l0, _):
        at = pl.multiple_of(l0 * 128, 128)
        right = jnp.concatenate(
            [half[pl.ds(at, 128), :], half[pl.ds(16384 + at, 128), :]], axis=1
        ).astype(BF)
        got = dot(over_x[pl.ds(pl.multiple_of(l0 * 32, 32), 32), :], right)
        got = got[:16] + got[16:]
        for side in range(2):
            for q in range(2):
                pixels[pl.ds(side * 2048 + 2 * l0 + q, 8, stride=256), :] = got[
                    8 * q : 8 * q + 8, 128 * side : 128 * side + 128
                ]
        return 0

    lax.fori_loop(0, 128, over_offsets, 0, unroll=4)
    out[:, :128] = pixels[:2048, :].astype(out.dtype)
    out[:, 128:] = pixels[2048:4096, :].astype(out.dtype)


def grid_and_rows(recv, table, weight, over_r, over_x, dtype):
    vmem = pl.BlockSpec(memory_space=pltpu.VMEM)
    return pl.pallas_call(
        grid_body,
        out_shape=jax.ShapeDtypeStruct((2048, 256), dtype),
        in_specs=[vmem] * 5,
        out_specs=vmem,
        scratch_shapes=[
            pltpu.VMEM((512 * S, 128), F32),
            pltpu.VMEM((2 * 128 * 128, 128), F32),
            pltpu.VMEM((ALL, 128), F32),
            pltpu.VMEM((ALL, 128), F32),
            pltpu.VMEM((NT, 128), jnp.int32),
            pltpu.SMEM((NT, 128), jnp.int32),
            pltpu.SemaphoreType.DMA,
        ],
        compiler_params=pltpu.CompilerParams(vmem_limit_bytes=56 * MIB),
        name="grid_and_rows",
    )(recv, table, weight, over_r, over_x)


def finish_body(
    pixels, over_t, over_v, out, recv, wide, middle, fold, last, send_a, recv_a, send_b, recv_b
):
    me = lax.axis_index("tile")
    chan = lax.axis_index("chan")
    home = me // 8
    stays = home == chan
    barrier = pltpu.get_barrier_semaphore()

    def greet(i, _):
        pl.semaphore_signal(
            barrier, inc=1, device_id=(lax.rem(me + i, NT), chan), device_id_type=MESH
        )
        return 0

    lax.fori_loop(1, NT, greet, 0)

    def greet_source(i, _):
        from_t, from_c = chan * 8 + i // NC, lax.rem(i, NC)

        @pl.when(jnp.logical_or(from_t != me, from_c != chan))
        def _():
            pl.semaphore_signal(barrier, inc=1, device_id=(from_t, from_c), device_id_type=MESH)

        return 0

    lax.fori_loop(0, NT, greet_source, 0)
    pl.semaphore_wait(barrier, jnp.where(stays, 2 * NT - 2, 2 * NT - 1))

    def copy(i):
        to = lax.rem(me + i, NT)
        return pltpu.make_async_remote_copy(
            src_ref=pixels.at[pl.ds(pl.multiple_of(to * 64, 64), 64)],
            dst_ref=recv.at[pl.ds(pl.multiple_of(me * 64, 64), 64)],
            send_sem=send_a.at[i],
            recv_sem=recv_a.at[i],
            device_id=(to, chan),
            device_id_type=MESH,
        )

    def start(i, _):
        copy(i).start()
        return 0

    lax.fori_loop(1, NT, start, 0)
    own = pl.ds(pl.multiple_of(me * 64, 64), 64)
    recv[own, :] = pixels[own, :]

    def wait(i, _):
        copy(i).wait()
        return 0

    lax.fori_loop(1, NT, wait, 0)
    for side in range(2):
        wide[side * 2048 : side * 2048 + 2048, :] = recv[
            :, 128 * side : 128 * side + 128
        ].astype(F32)

    def over_tiles(l, _):
        rows = [
            jnp.concatenate(
                [wide[pl.ds(side * 2048 + 2 * l + q, NT, stride=64), :] for side in range(2)],
                axis=1,
            )
            for q in range(2)
        ]
        got = dot(over_t[...], jnp.concatenate(rows, axis=0).astype(BF))
        got = got[:64] + got[64:]
        at = pl.multiple_of(l * 64, 64)
        middle[pl.ds(at, 64), :] = got[:, :128]
        middle[pl.ds(2048 + at, 64), :] = got[:, 128:]
        return 0

    lax.fori_loop(0, 32, over_tiles, 0, unroll=2)

    def over_columns(a, _):
        made = []
        for b in range(4):
            m0 = b * 8 + a
            right = jnp.concatenate(
                [
                    middle[pl.ds(side * 2048 + 32 * q + m0, 32, stride=64), :]
                    for q in range(2)
                    for side in range(2)
                ],
                axis=1,
            )
            high = right.astype(BF)
            low = (right - high.astype(F32)).astype(BF)
            left = over_v[pl.ds(pl.multiple_of(m0 * 64, 64), 64), :]
            got = dot_t(left, high)
            made.append(got[:32] + got[32:] + dot_t(left[:32], low))
        fold[pl.ds(a, 32, stride=8), :] = jnp.concatenate(made, axis=1)
        return 0

    lax.fori_loop(0, 8, over_columns, 0)
    slot = lax.rem(me, 8) * NC + chan

    def give(i):
        to = lax.rem(me + i, NT)
        return pltpu.make_async_remote_copy(
            src_ref=fold.at[pl.ds(pl.multiple_of(to * 8, 8), 8)],
            dst_ref=last.at[pl.ds(pl.multiple_of(slot * 8, 8), 8)],
            send_sem=send_b.at[i],
            recv_sem=recv_b.at[slot],
            device_id=(to, home),
            device_id_type=MESH,
        )

    def take(i):
        at = pl.ds(pl.multiple_of(i * 8, 8), 8)
        return pltpu.make_async_remote_copy(
            src_ref=last.at[at],
            dst_ref=last.at[at],
            send_sem=send_b.at[i],
            recv_sem=recv_b.at[i],
            device_id=(chan * 8 + i // NC, lax.rem(i, NC)),
            device_id_type=MESH,
        )

    @pl.when(jnp.logical_not(stays))
    def _():
        give(0).start()

    @pl.when(stays)
    def _():
        last[pl.ds(pl.multiple_of(slot * 8, 8), 8), :] = fold[
            pl.ds(pl.multiple_of(me * 8, 8), 8), :
        ]

    def start_b(i, _):
        give(i).start()
        return 0

    lax.fori_loop(1, NT, start_b, 0)

    def wait_b(i, _):
        @pl.when(jnp.logical_or(jnp.logical_not(stays), i != slot))
        def _():
            take(i).wait_recv()

        return 0

    lax.fori_loop(0, NT, wait_b, 0)

    @pl.when(jnp.logical_not(stays))
    def _():
        give(0).wait_send()

    def sent_b(i, _):
        give(i).wait_send()
        return 0

    lax.fori_loop(1, NT, sent_b, 0)
    for t in range(8):
        total = last[t * 32 : t * 32 + 8, :]
        for c in range(1, NC):
            total = total + last[t * 32 + c * 8 : t * 32 + c * 8 + 8, :]
        out[t * 8 : t * 8 + 8, :] = total


def finish(pixels, over_t, over_v):
    vmem = pl.BlockSpec(memory_space=pltpu.VMEM)
    return pl.pallas_call(
        finish_body,
        out_shape=jax.ShapeDtypeStruct((64, 128), F32),
        in_specs=[vmem] * 3,
        out_specs=vmem,
        scratch_shapes=[
            pltpu.VMEM((2048, 256), BF),
            pltpu.VMEM((4096, 128), F32),
            pltpu.VMEM((4096, 128), F32),
            pltpu.VMEM((256, 128), F32),
            pltpu.VMEM((256, 128), F32),
            pltpu.SemaphoreType.DMA((NT,)),
            pltpu.SemaphoreType.DMA((NT,)),
            pltpu.SemaphoreType.DMA((NT,)),
            pltpu.SemaphoreType.DMA((NT,)),
        ],
        compiler_params=pltpu.CompilerParams(
            collective_id=1, has_side_effects=True, vmem_limit_bytes=32 * MIB
        ),
        name="finish",
    )(pixels, over_t, over_v)


def local(visibilities, kernels, destination, cell, plane):
    over_r, over_x = (jnp.asarray(t) for t in row_tables())
    over_t, over_v = (jnp.asarray(t) for t in column_tables())
    samples = visibilities[0]
    dest = destination.reshape(1, BLK)
    kern = kernels.reshape(NW * 128, 128)
    none = jnp.zeros((1, BLK), jnp.int32)
    recv, table, weight, most = exchange(True, samples, dest, cell, plane, none, kern)
    largest = lax.pmax(most[0, 0], ("tile", "chan"))
    pixels = grid_and_rows(recv, table, weight, over_r, over_x, BF)

    def more(pixels):
        def again(state):
            done, total = state
            more_recv = exchange(
                False, samples, dest, cell, plane, jnp.broadcast_to(done, (1, BLK))
            )[0]
            return done + CAP, total + grid_and_rows(
                more_recv, table, weight, over_r, over_x, F32
            )

        return lax.while_loop(
            lambda state: state[0].astype(F32) < largest,
            again,
            (jnp.int32(CAP), pixels.astype(F32)),
        )[1].astype(BF)

    pixels = lax.cond(largest > CAP, more, lambda p: p, pixels)
    out = finish(pixels, over_t, over_v)
    return out.reshape(8, 8, 4, 32).transpose(0, 3, 2, 1).reshape(256, 32)


def solution(mesh):
    placed = (
        P("chan", "tile", None),
        P("chan", None, None, None, None),
        P("chan", "tile", None),
        P("chan", "tile"),
        P("chan", "tile"),
    )
    return jax.shard_map(
        local, mesh=mesh, in_specs=placed, out_specs=P("chan", "tile"), check_vma=False
    )
```

time: 851 us -> 197 us (0.23)
  matrix products: 335 us -> 0 us
  other arithmetic: 271 us -> 0 us
  Pallas kernels: 0 us -> 125 us
  waiting for transfers between devices: 103 us -> 0 us
  local copies, waits for them, and re-layouts: 106 us -> 4.97 us
  blocking collectives: 0 us -> 65.6 us
  starting transfers between devices: 17 us -> 0 us
  between operations: 13.5 us -> 0.83 us
    dot_general x7 -> x0, matrix products: 335 us -> none  [the longest x1 140 us: local(): jnp.einsum('acxpy,cym->pmax', grid_round, sine.reshape(cell_cols, S, P_SI...]
    scatter-add x3 -> x0, other arithmetic: 158 us -> none  [add_block(): return (grid_cells.at[meta_blk // NW].add(patches), None)]
    pallas_call x0 -> x3, Pallas kernels: none -> 125 us  [the longest x1 70.1 us: grid_and_rows(): pl.pallas_call(grid_body, out_shape=jax.ShapeDtypeStruct((2048, 256), dty...]
    reduce_scatter x2 -> x0, waiting for transfers between devices: 103 us -> none  [the longest x1 81.3 us: local(): lax.psum_scatter(jnp.dot(transformed[0], own_cosine, preferred_element_ty...]
    pmax x0 -> x1, blocking collectives: none -> 65.6 us  [local(): largest = lax.pmax(most[0, 0], ('tile', 'chan'))]
    convert_element_type x5 -> x0, other arithmetic: 40.4 us -> none  [the longest x3 21.4 us: block_patches(): (vis_real * kern_real - vis_imag * kern_imag).astype(jnp.bfloat16)]
    scatter x2 -> x0, local copies, waits for them, and re-layouts: 39.3 us -> none  [the longest x1 26.6 us: local(): send_samples = jnp.zeros((tile_count, capacity, samples.shape[1]), jnp.fl...]
    reshape x2, local copies, waits for them, and re-layouts: 28.1 us -> 0.83 us  [local(): return out.reshape(8, 8, 4, 32).transpose(0, 3, 2, 1).reshape(256, 32)]
  transfers between devices with their start and end apart: 4 -> 0, of which waited for: 2 -> 0; matrix products, arithmetic and copies ran while one was open for 6% -> 0% of each run, Pallas kernels for 0% -> 0%
where the time goes in v1:
time: 197 us
  Pallas kernels  125 us (63%)
  blocking collectives  65.6 us (33%)
  local copies, waits for them, and re-layouts  4.97 us (3%)
    pallas_call x1, Pallas kernels, grid_and_rows(): pl.pallas_call(grid_body, out_shape=jax.ShapeDtypeStruct((2048, 256), dty...  70.1 us
    pmax x1, blocking collectives, local(): largest = lax.pmax(most[0, 0], ('tile', 'chan'))  65.6 us
    pallas_call x1, Pallas kernels, finish(): pl.pallas_call(finish_body, out_shape=jax.ShapeDtypeStruct((64, 128), F32...  39.9 us
    pallas_call x1, Pallas kernels, exchange(): pl.pallas_call(functools.partial(exchange_body, first), out_shape=shapes,...  15.5 us

profile of v1, /device:TPU:1, one launch (start us, length us, event | category | flops | bytes accessed | tf_op | source)
XLA Modules:
  0.0 196.9 jit_solution(10177656176691726856)
XLA Ops:
  0.0 0.0 copy-start.2
  0.0 1.2 copy-done.2
  1.2 15.5 %exchange.1 = (bf16[1024,128]{1,0:T(8,128)(2,1)S(1)}, f32[4096,128]{1,0:T(8,128)S(1)}, bf16[4096,128]{1,0:T(8,128)(2,1)}, f32[8,128]{1,0:T(8,128)S(1)}) custom-call(f32[256,128]{1,0:T(8,128)} %bitcast.10, s32[1,256]{1,0:T(1,128)} %bitcast.13, s32[1,256]{1,0:T(1,128)} %cell.1, s32[1,256]{1,0:T(1,128)} %plane.1, s32[1,256]{1,0:T(1,128)S(1)} %broadcast_in_dim.6.skipped, ...), custom_call_target="tpu_custom_call" | custom-call | tf_op jit(solution)/shard_map/exchange/pallas_call | solution.py:172
  16.8 0.0 copy-start.3
  16.8 0.7 copy-done.3
  17.5 0.0 copy-start.7
  17.5 0.5 slice.3
  18.0 65.6 %pmax.7 = f32[]{:T(128)} all-reduce(f32[]{:T(128)} %bitcast.3), channel_id=1, replica_groups=mesh['tile'=32,'chan'=4] {'tile','chan'}, use_global_device_ids=true, to_apply=%region_0.0 | all-reduce | flops 1 | bytes 8 | tf_op jit(solution)/shard_map/pmax | solution.py:485
  84.3 0.0 copy-start.8
  84.3 0.0 copy-start.9
  84.3 0.0 copy-start.10
  84.3 0.0 copy-start.11
  84.3 0.0 copy-start.12
  84.4 0.0 copy-start.13
  84.4 70.1 %grid_and_rows.2 = bf16[2048,256]{1,0:T(8,128)(2,1)} custom-call(bf16[1024,128]{1,0:T(8,128)(2,1)} %copy-done.3, f32[4096,128]{1,0:T(8,128)S(1)} %get-tuple-element.103.table, bf16[4096,128]{1,0:T(8,128)(2,1)} %get-tuple-element.104.weight, bf16[256,256]{1,0:T(8,128)(2,1)} %constant.16.clone.over_r, bf16[4096,128]{1,0:T(8,128)(2,1)} %constant.17.clone.over_x), custom_call_target="tpu_custom_call" | custom-call | tf_op jit(solution)/shard_map/grid_and_rows/pallas_call | solution.py:272
  154.5 0.0 copy-done.7
  154.5 0.0 copy-done.8
  154.5 0.0 copy-done.9
  154.5 0.0 copy-done.10
  154.5 0.0 copy-done.11
  154.5 0.0 copy-done.12
  154.5 0.0 copy-done.13
  154.5 0.0 copy-start.1
  154.5 0.0 copy-start.4
  154.6 1.6 copy-done.1
  156.1 0.0 copy-done.4
  156.1 39.9 %finish.1 = f32[64,128]{1,0:T(8,128)S(1)} custom-call(bf16[2048,256]{1,0:T(8,128)(2,1)} %get-tuple-element.231.pixels, bf16[128,64]{1,0:T(8,128)(2,1)S(1)} %copy-done.4, bf16[2048,512]{1,0:T(8,128)(2,1)S(1)} %copy-done.1), custom_call_target="tpu_custom_call" | custom-call | tf_op jit(solution)/shard_map/finish/pallas_call | solution.py:454
  196.0 0.1 reshape.14
  196.1 0.1 copy.10
  196.2 0.7 reshape.15
  (2 shorter events, 0.0 us)
Async XLA Ops:
  0.0 1.2 copy-start.2
  16.8 0.7 copy-start.3
  17.5 137.0 %copy-start.7 = (f32[4096,128]{1,0:T(8,128)}, f32[4096,128]{1,0:T(8,128)S(1)}, u32[]{:S(2)}) copy-start(f32[4096,128]{1,0:T(8,128)S(1)} %get-tuple-element.103.table) | copy-start | bytes 6291460
  84.3 70.2 %copy-start.8 = (bf16[4096,128]{1,0:T(8,128)(2,1)S(1)}, bf16[4096,128]{1,0:T(8,128)(2,1)}, u32[]{:S(2)}) copy-start(bf16[4096,128]{1,0:T(8,128)(2,1)} %constant.17.clone.over_x) | copy-start | bytes 3145732
  84.3 70.2 %copy-start.9 = (f32[1,256,128]{2,1,0:T(8,128)S(1)}, f32[1,256,128]{2,1,0:T(8,128)}, u32[]{:S(2)}) copy-start(f32[1,256,128]{2,1,0:T(8,128)} %param.13) | copy-start | bytes 393220
  84.3 70.2 %copy-start.10 = (bf16[256,256]{1,0:T(8,128)(2,1)S(1)}, bf16[256,256]{1,0:T(8,128)(2,1)}, u32[]{:S(2)}) copy-start(bf16[256,256]{1,0:T(8,128)(2,1)} %constant.16.clone.over_r) | copy-start | bytes 393220
  84.3 70.2 %copy-start.11 = (s32[1,256,1]{1,2,0:T(1,128)S(1)}, s32[1,256,1]{1,2,0:T(1,128)}, u32[]{:S(2)}) copy-start(s32[1,256,1]{1,2,0:T(1,128)} %param.15) | copy-start | bytes 3076
  84.3 70.2 %copy-start.12 = (s32[1,256]{1,0:T(1,128)S(1)}, s32[1,256]{1,0:T(1,128)}, u32[]{:S(2)}) copy-start(s32[1,256]{1,0:T(1,128)} %cell.1) | copy-start | bytes 3076
  84.4 70.2 %copy-start.13 = (s32[1,256]{1,0:T(1,128)S(1)}, s32[1,256]{1,0:T(1,128)}, u32[]{:S(2)}) copy-start(s32[1,256]{1,0:T(1,128)} %plane.1) | copy-start | bytes 3076
  154.5 1.6 copy-start.1
  154.5 1.6 copy-start.4

commit v2 on v1

--- a/solution.py
+++ b/solution.py
@@ -18,6 +18,10 @@
 NC = 4
 BLK = 256
 CAP = 31
+GS = 65
+HS = 129
+TOGETHER = 32
+WS = 65
 SLOTS = 32
 ALL = NT * SLOTS
 MIB = 1 << 20
@@ -90,19 +94,24 @@
     value = jnp.where(kind == 0, row, jnp.where(kind == 1, plane, jnp.where(kind == 2, inner, 1)))
     held = jnp.logical_and(here, jnp.logical_or(kind == 3, jnp.bitwise_and(lane, 31) == rank))
     facts = dot_t(one_b, jnp.where(held, value.astype(F32), 0.0).astype(BF))
+    named_most = jnp.max(jnp.sum(one, axis=1, keepdims=True), axis=0, keepdims=True)
+    facts = jnp.where(iota((NT, 128), 1) < 112, facts, named_most)
     last = jnp.where(iota((ALL, NT), 0) == iota((ALL, NT), 1) * SLOTS + CAP, 1.0, 0.0).astype(BF)
     slots = dot(pick, samples.astype(BF)) + dot(last, facts.astype(BF))
-    return slots.astype(BF), jnp.sum(one, axis=1, keepdims=True)
+    return slots.astype(BF)
 
 
 def exchange_body(first, samples, dest, cell, plane, skipped, *rest):
     if first:
-        kern, recv, table, weight, most, send, send_sem, recv_sem = rest
+        kern_hbm, recv, facts, table, weight, most, send, send_sem, recv_sem, kern, mine, seen, kern_sem, send_y, recv_y = rest
     else:
-        recv, send, send_sem, recv_sem = rest
+        recv, facts, send, send_sem, recv_sem = rest
     me = lax.axis_index("tile")
     chan = lax.axis_index("chan")
     barrier = pltpu.get_barrier_semaphore()
+    fetch = pltpu.make_async_copy(kern_hbm, kern, kern_sem) if first else None
+    if first:
+        fetch.start()
 
     def greet(i, _):
         pl.semaphore_signal(
@@ -111,9 +120,13 @@
         return 0
 
     lax.fori_loop(1, NT, greet, 0)
-    slots, named = fill_slots(samples[...], dest[...], cell[...], plane[...], skipped[...])
-    send[...] = slots
-    pl.semaphore_wait(barrier, NT - 1)
+    if first:
+        for i in range(1, NC):
+            pl.semaphore_signal(
+                barrier, inc=1, device_id=(me, lax.rem(chan + i, NC)), device_id_type=MESH
+            )
+    send[...] = fill_slots(samples[...], dest[...], cell[...], plane[...], skipped[...])
+    pl.semaphore_wait(barrier, NT + NC - 2 if first else NT - 1)
 
     def copy(i):
         to = lax.rem(me + i, NT)
@@ -134,14 +147,13 @@
     own = pl.ds(pl.multiple_of(me * SLOTS, SLOTS), SLOTS)
     recv[own, :] = send[own, :]
     if first:
-        most[...] = jnp.broadcast_to(jnp.max(named, axis=0, keepdims=True), (8, 128))
         low = iota((S, 128), 1) < S
 
         def prepare(w, _):
-            both = kern[pl.ds(pl.multiple_of(w * 128, 128), 128), :].astype(F32)
+            base = pl.multiple_of(w * 128, 128)
+            both = kern[pl.ds(base, 128), :].astype(F32)
             real, imag = both[:S], both[S:]
             turned = both.T[:S]
-            base = pl.multiple_of(w * 128, 128)
             table[pl.ds(base, S), :] = turned
             swapped = pltpu.roll(turned, S, 1)
             table[pl.ds(base + S, S), :] = jnp.where(low, -swapped, swapped)
@@ -149,19 +161,53 @@
             weight[pl.ds(base + S, S), :] = jnp.where(low, -pltpu.roll(imag, S, 1), real).astype(BF)
             return 0
 
-        lax.fori_loop(0, NW, prepare, 0)
+        fetch.wait()
+        lax.fori_loop(0, 24, prepare, 0, unroll=2)
 
     def wait(i, _):
         copy(i).wait()
         return 0
 
     lax.fori_loop(1, NT, wait, 0)
+    last = jnp.where(iota((NT, ALL), 1) == iota((NT, ALL), 0) * SLOTS + CAP, 1.0, 0.0).astype(BF)
+    raw = dot(last, recv[...])
+    lane = iota((NT, 128), 1)
+    code = (pltpu.roll(raw, 64, 1) * 128.0 + raw) * 32.0 + pltpu.roll(raw, 96, 1)
+    facts[...] = jnp.where(lane < SLOTS, code, raw).astype(jnp.int32)
+    if first:
+        largest = jnp.max(jnp.where(lane < 112, 0.0, raw), axis=0, keepdims=True)
+        largest = jnp.broadcast_to(jnp.max(largest, axis=1, keepdims=True), (8, 128))
+        mine[...] = largest
+
+        def tell(i):
+            return pltpu.make_async_remote_copy(
+                src_ref=mine,
+                dst_ref=seen.at[i],
+                send_sem=send_y.at[i],
+                recv_sem=recv_y.at[i],
+                device_id=(me, lax.rem(chan + i, NC)),
+                device_id_type=MESH,
+            )
+
+        for i in range(1, NC):
+            tell(i).start()
+        lax.fori_loop(24, NW, prepare, 0, unroll=2)
+        for i in range(1, NC):
+            tell(i).wait()
+            largest = jnp.maximum(largest, seen[i])
+        most[...] = largest
 
 
 def exchange(first, samples, dest, cell, plane, skipped, kern=None):
     vmem = pl.BlockSpec(memory_space=pltpu.VMEM)
-    shapes = [jax.ShapeDtypeStruct((ALL, 128), BF)]
+    shapes = [jax.ShapeDtypeStruct((ALL, 128), BF), jax.ShapeDtypeStruct((NT, 128), jnp.int32)]
     operands = [samples, dest, cell, plane, skipped]
+    specs = [vmem] * 5
+    scratch = [
+        pltpu.VMEM((ALL, 128), BF),
+        pltpu.SemaphoreType.DMA((NT,)),
+        pltpu.SemaphoreType.DMA((NT,)),
+    ]
     if first:
         shapes += [
             jax.ShapeDtypeStruct((NW * 128, 128), F32),
@@ -169,16 +215,21 @@
             jax.ShapeDtypeStruct((8, 128), F32),
         ]
         operands.append(kern)
+        specs.append(pl.BlockSpec(memory_space=pltpu.HBM))
+        scratch += [
+            pltpu.VMEM((NW * 128, 128), BF),
+            pltpu.VMEM((8, 128), F32),
+            pltpu.VMEM((NC, 8, 128), F32),
+            pltpu.SemaphoreType.DMA,
+            pltpu.SemaphoreType.DMA((NC,)),
+            pltpu.SemaphoreType.DMA((NC,)),
+        ]
     return pl.pallas_call(
         functools.partial(exchange_body, first),
         out_shape=shapes,
-        in_specs=[vmem] * len(operands),
+        in_specs=specs,
         out_specs=[vmem] * len(shapes),
-        scratch_shapes=[
-            pltpu.VMEM((ALL, 128), BF),
-            pltpu.SemaphoreType.DMA((NT,)),
-            pltpu.SemaphoreType.DMA((NT,)),
-        ],
+        scratch_shapes=scratch,
         compiler_params=pltpu.CompilerParams(
             collective_id=0 if first else 2, has_side_effects=True, vmem_limit_bytes=32 * MIB
         ),
@@ -186,72 +237,74 @@
     )(*operands)
 
 
-def grid_body(
-    recv, table, weight, over_r, over_x, out, grid, half, fill_a, fill_b, facts_v, facts, sem
-):
+def grid_body(facts, recv, table, weight, over_r, over_x, out, grid, half, fill_a, fill_b, todo):
     lane = iota((ALL, 128), 1)
     slot = iota((ALL, 128), 0)
     blocks = jnp.where(jnp.bitwise_and(slot, SLOTS - 1) == CAP, 0.0, recv[...].astype(F32))
     swapped = pltpu.roll(blocks, S, 1)
     fill_a[...] = jnp.where(lane < S, blocks, swapped)
     fill_b[...] = jnp.where(lane < S, swapped, blocks)
-    last = jnp.where(iota((NT, ALL), 1) == iota((NT, ALL), 0) * SLOTS + CAP, 1.0, 0.0).astype(BF)
-    raw = dot(last, recv[...])
-    code = (pltpu.roll(raw, 64, 1) * 128.0 + raw) * 32.0 + pltpu.roll(raw, 96, 1)
-    facts_v[...] = jnp.where(iota((NT, 128), 1) < SLOTS, code, raw).astype(jnp.int32)
-    to_scalar = pltpu.make_async_copy(facts_v, facts, sem)
-    to_scalar.start()
 
     def clear(i, _):
         grid[pl.ds(pl.multiple_of(i * 512, 512), 512), :] = jnp.zeros((512, 128), F32)
         return 0
 
-    lax.fori_loop(0, 64, clear, 0)
-    to_scalar.wait()
-
-    def from_source(t, _):
-        def four(j, _):
-            made = []
-            for k in range(4):
-                i = j * 4 + k
-                fact = facts[t, i]
-                w = jnp.bitwise_and(fact, 31)
-                base = pl.multiple_of(w * 128, 128)
-                i = t * SLOTS + i
-                left = (
-                    fill_a[pl.ds(i, 1), :] * table[pl.ds(base, S), :]
-                    + fill_b[pl.ds(i, 1), :] * table[pl.ds(base + S, S), :]
-                ).astype(BF)
-                patch = dot(left, weight[pl.ds(base, 128), :])
-                made.append((lax.shift_right_logical(fact, 5), patch))
-            for place, patch in made:
-                at = pl.ds(pl.multiple_of(place * S, S), S)
-                grid[at, :] = grid[at, :] + patch
+    lax.fori_loop(0, GS, clear, 0)
+
+    def from_source(t, at):
+        number = facts[t, 96]
+
+        def eight(j, _):
+            for k in range(8):
+                i = j * 8 + k
+                todo[at + i] = facts[t, i] * ALL + t * SLOTS + i
             return 0
 
-        lax.fori_loop(0, lax.shift_right_logical(facts[t, 96] + 3, 2), four, 0)
-        return 0
-
-    lax.fori_loop(0, NT, from_source, 0)
+        lax.fori_loop(0, lax.shift_right_logical(number + 7, 3), eight, 0)
+        return at + number
+
+    number = lax.fori_loop(0, NT, from_source, 0)
+    for k in range(TOGETHER):
+        todo[number + k] = CAP
+
+    def blocks_together(j, _):
+        made = []
+        for k in range(TOGETHER):
+            code = todo[j * TOGETHER + k]
+            i = jnp.bitwise_and(code, ALL - 1)
+            fact = lax.shift_right_logical(code, 10)
+            base = pl.multiple_of(jnp.bitwise_and(fact, 31) * 128, 128)
+            left = (
+                fill_a[pl.ds(i, 1), :] * table[pl.ds(base, S), :]
+                + fill_b[pl.ds(i, 1), :] * table[pl.ds(base + S, S), :]
+            ).astype(BF)
+            patch = dot(left, weight[pl.ds(base, 128), :])
+            made.append((lax.shift_right_logical(fact, 5), patch))
+        for place, patch in made:
+            at = pl.ds(place * GS, S)
+            grid[at, :] = grid[at, :] + patch
+        return 0
+
+    lax.fori_loop(0, (number + TOGETHER - 1) // TOGETHER, blocks_together, 0)
 
     def over_rows(x, _):
-        part = [grid[pl.ds(i * 8192 + x, 128, stride=S), :] for i in range(4)]
+        part = [grid[pl.ds(i * 128 * GS + x, 128, stride=GS), :] for i in range(4)]
         real = jnp.concatenate([p[:, :S] for p in part], axis=1)
         imag = jnp.concatenate([p[:, S:] for p in part], axis=1)
         got = dot(over_r[...], jnp.concatenate([real, imag], axis=0).astype(BF))
-        half[pl.ds(x, 128, stride=128), :] = got[:128, :128]
-        half[pl.ds(S + x, 128, stride=128), :] = got[128:, :128]
-        half[pl.ds(16384 + x, 128, stride=128), :] = got[:128, 128:]
-        half[pl.ds(16384 + S + x, 128, stride=128), :] = got[128:, 128:]
-        return 0
-
-    lax.fori_loop(0, S, over_rows, 0)
+        half[pl.ds(x, 128, stride=HS), :] = got[:128, :128]
+        half[pl.ds(S + x, 128, stride=HS), :] = got[128:, :128]
+        half[pl.ds(128 * HS + x, 128, stride=HS), :] = got[:128, 128:]
+        half[pl.ds(128 * HS + S + x, 128, stride=HS), :] = got[128:, 128:]
+        return 0
+
+    lax.fori_loop(0, S, over_rows, 0, unroll=8)
     pixels = grid
 
     def over_offsets(l0, _):
-        at = pl.multiple_of(l0 * 128, 128)
+        at = pl.multiple_of(l0 * HS, 1)
         right = jnp.concatenate(
-            [half[pl.ds(at, 128), :], half[pl.ds(16384 + at, 128), :]], axis=1
+            [half[pl.ds(at, 128), :], half[pl.ds(128 * HS + at, 128), :]], axis=1
         ).astype(BF)
         got = dot(over_x[pl.ds(pl.multiple_of(l0 * 32, 32), 32), :], right)
         got = got[:16] + got[16:]
@@ -262,35 +315,49 @@
                 ]
         return 0
 
-    lax.fori_loop(0, 128, over_offsets, 0, unroll=4)
+    lax.fori_loop(0, 128, over_offsets, 0, unroll=16)
     out[:, :128] = pixels[:2048, :].astype(out.dtype)
     out[:, 128:] = pixels[2048:4096, :].astype(out.dtype)
 
 
-def grid_and_rows(recv, table, weight, over_r, over_x, dtype):
+def grid_and_rows(facts, recv, table, weight, over_r, over_x, dtype):
     vmem = pl.BlockSpec(memory_space=pltpu.VMEM)
     return pl.pallas_call(
         grid_body,
         out_shape=jax.ShapeDtypeStruct((2048, 256), dtype),
-        in_specs=[vmem] * 5,
+        in_specs=[pl.BlockSpec(memory_space=pltpu.SMEM)] + [vmem] * 5,
         out_specs=vmem,
         scratch_shapes=[
-            pltpu.VMEM((512 * S, 128), F32),
-            pltpu.VMEM((2 * 128 * 128, 128), F32),
+            pltpu.VMEM((512 * GS, 128), F32),
+            pltpu.VMEM((2 * 128 * HS, 128), F32),
             pltpu.VMEM((ALL, 128), F32),
             pltpu.VMEM((ALL, 128), F32),
-            pltpu.VMEM((NT, 128), jnp.int32),
-            pltpu.SMEM((NT, 128), jnp.int32),
-            pltpu.SemaphoreType.DMA,
+            pltpu.SMEM((ALL + 64,), jnp.int32),
         ],
         compiler_params=pltpu.CompilerParams(vmem_limit_bytes=56 * MIB),
         name="grid_and_rows",
-    )(recv, table, weight, over_r, over_x)
+    )(facts, recv, table, weight, over_r, over_x)
 
 
 def finish_body(
-    pixels, over_t, over_v, out, recv, wide, middle, fold, last, send_a, recv_a, send_b, recv_b
+    pixels,
+    over_t,
+    over_v_hbm,
+    out,
+    recv,
+    wide,
+    middle,
+    fold,
+    last,
+    over_v,
+    send_a,
+    recv_a,
+    send_b,
+    recv_b,
+    table_sem,
 ):
+    fetch = pltpu.make_async_copy(over_v_hbm, over_v, table_sem)
+    fetch.start()
     me = lax.axis_index("tile")
     chan = lax.axis_index("chan")
     home = me // 8
@@ -341,27 +408,31 @@
         return 0
 
     lax.fori_loop(1, NT, wait, 0)
-    for side in range(2):
-        wide[side * 2048 : side * 2048 + 2048, :] = recv[
-            :, 128 * side : 128 * side + 128
-        ].astype(F32)
+
+    def widen(t, _):
+        block = recv[pl.ds(pl.multiple_of(t * 64, 64), 64), :].astype(F32)
+        wide[pl.ds(t * WS, 64), :] = block[:, :128]
+        wide[pl.ds((NT + t) * WS, 64), :] = block[:, 128:]
+        return 0
+
+    lax.fori_loop(0, NT, widen, 0, unroll=4)
 
     def over_tiles(l, _):
         rows = [
             jnp.concatenate(
-                [wide[pl.ds(side * 2048 + 2 * l + q, NT, stride=64), :] for side in range(2)],
+                [wide[pl.ds(side * NT * WS + 2 * l + q, NT, stride=WS), :] for side in range(2)],
                 axis=1,
             )
             for q in range(2)
         ]
         got = dot(over_t[...], jnp.concatenate(rows, axis=0).astype(BF))
         got = got[:64] + got[64:]
-        at = pl.multiple_of(l * 64, 64)
-        middle[pl.ds(at, 64), :] = got[:, :128]
-        middle[pl.ds(2048 + at, 64), :] = got[:, 128:]
-        return 0
-
-    lax.fori_loop(0, 32, over_tiles, 0, unroll=2)
+        middle[pl.ds(l * WS, 64), :] = got[:, :128]
+        middle[pl.ds((32 + l) * WS, 64), :] = got[:, 128:]
+        return 0
+
+    lax.fori_loop(0, 32, over_tiles, 0, unroll=8)
+    fetch.wait()
 
     def over_columns(a, _):
         made = []
@@ -369,7 +440,7 @@
             m0 = b * 8 + a
             right = jnp.concatenate(
                 [
-                    middle[pl.ds(side * 2048 + 32 * q + m0, 32, stride=64), :]
+                    middle[pl.ds(side * 32 * WS + 32 * q + m0, 32, stride=WS), :]
                     for q in range(2)
                     for side in range(2)
                 ],
@@ -383,7 +454,7 @@
         fold[pl.ds(a, 32, stride=8), :] = jnp.concatenate(made, axis=1)
         return 0
 
-    lax.fori_loop(0, 8, over_columns, 0)
+    lax.fori_loop(0, 8, over_columns, 0, unroll=4)
     slot = lax.rem(me, 8) * NC + chan
 
     def give(i):
@@ -454,18 +525,20 @@
     return pl.pallas_call(
         finish_body,
         out_shape=jax.ShapeDtypeStruct((64, 128), F32),
-        in_specs=[vmem] * 3,
+        in_specs=[vmem] * 2 + [pl.BlockSpec(memory_space=pltpu.HBM)],
         out_specs=vmem,
         scratch_shapes=[
             pltpu.VMEM((2048, 256), BF),
-            pltpu.VMEM((4096, 128), F32),
-            pltpu.VMEM((4096, 128), F32),
+            pltpu.VMEM((2 * NT * WS, 128), F32),
+            pltpu.VMEM((2 * 32 * WS, 128), F32),
             pltpu.VMEM((256, 128), F32),
             pltpu.VMEM((256, 128), F32),
+            pltpu.VMEM((2048, 512), BF),
             pltpu.SemaphoreType.DMA((NT,)),
             pltpu.SemaphoreType.DMA((NT,)),
             pltpu.SemaphoreType.DMA((NT,)),
             pltpu.SemaphoreType.DMA((NT,)),
+            pltpu.SemaphoreType.DMA,
         ],
         compiler_params=pltpu.CompilerParams(
             collective_id=1, has_side_effects=True, vmem_limit_bytes=32 * MIB
@@ -481,18 +554,18 @@
     dest = destination.reshape(1, BLK)
     kern = kernels.reshape(NW * 128, 128)
     none = jnp.zeros((1, BLK), jnp.int32)
-    recv, table, weight, most = exchange(True, samples, dest, cell, plane, none, kern)
-    largest = lax.pmax(most[0, 0], ("tile", "chan"))
-    pixels = grid_and_rows(recv, table, weight, over_r, over_x, BF)
+    recv, facts, table, weight, most = exchange(True, samples, dest, cell, plane, none, kern)
+    largest = most[0, 0]
+    pixels = grid_and_rows(facts, recv, table, weight, over_r, over_x, BF)
 
     def more(pixels):
         def again(state):
             done, total = state
-            more_recv = exchange(
+            more_recv, more_facts = exchange(
                 False, samples, dest, cell, plane, jnp.broadcast_to(done, (1, BLK))
-            )[0]
+            )
             return done + CAP, total + grid_and_rows(
-                more_recv, table, weight, over_r, over_x, F32
+                more_facts, more_recv, table, weight, over_r, over_x, F32
             )
 
         return lax.while_loop(

time: 197 us -> 77.9 us (0.40)
  blocking collectives: 65.6 us -> 0 us
  Pallas kernels: 125 us -> 71.1 us
    pmax x1 -> x0, blocking collectives: 65.6 us -> none  [local(): largest = lax.pmax(most[0, 0], ('tile', 'chan'))]
    pallas_call x1, Pallas kernels: 70.1 us -> 16.5 us  [grid_and_rows(): pl.pallas_call(grid_body, out_shape=jax.ShapeDtypeStruct((2048, 256), dty...]
    pallas_call x1, Pallas kernels: 39.9 us -> 34.5 us  [finish(): pl.pallas_call(finish_body, out_shape=jax.ShapeDtypeStruct((64, 128), F32...]
    pallas_call x1, Pallas kernels: 15.5 us -> 20.1 us  [exchange(): pl.pallas_call(functools.partial(exchange_body, first), out_shape=shapes,...]
    unnamed x22 -> x24, local copies, waits for them, and re-layouts: 3.52 us -> 4.12 us
where the time goes in v2:
time: 77.9 us; the launch traced here: 77.4 us
  Pallas kernels  71.1 us (91%)
  local copies, waits for them, and re-layouts  5.53 us (7%)
    pallas_call x1, Pallas kernels, finish(): pl.pallas_call(finish_body, out_shape=jax.ShapeDtypeStruct((64, 128), F32...  34.5 us
    pallas_call x1, Pallas kernels, exchange(): pl.pallas_call(functools.partial(exchange_body, first), out_shape=shapes,...  20.1 us
    pallas_call x1, Pallas kernels, grid_and_rows(): pl.pallas_call(grid_body, out_shape=jax.ShapeDtypeStruct((2048, 256), dty...  16.5 us
    unnamed x24, local copies, waits for them, and re-layouts  4.12 us

profile of v2, /device:TPU:1, one launch (start us, length us, event | category | flops | bytes accessed | tf_op | source)
XLA Modules:
  0.0 77.4 jit_solution(3777056624016068927)
XLA Ops:
  0.0 0.0 copy-start.2
  0.0 1.2 %copy-done.2 = bf16[1,32,2,64,128]{4,3,2,1,0:T(8,128)(2,1)S(1)} copy-done((bf16[1,32,2,64,128]{4,3,2,1,0:T(8,128)(2,1)S(1)}, bf16[1,32,2,64,128]{4,3,2,1,0:T(8,128)(2,1)}, u32[]{:S(2)}) %copy-start.2) | copy-done | bytes 1048600
  1.2 20.1 %exchange.1 = (bf16[1024,128]{1,0:T(8,128)(2,1)S(1)}, s32[32,128]{1,0:T(8,128)S(1)}, f32[4096,128]{1,0:T(8,128)S(1)}, bf16[4096,128]{1,0:T(8,128)(2,1)}, f32[8,128]{1,0:T(8,128)S(1)}) custom-call(f32[256,128]{1,0:T(8,128)} %bitcast.10, s32[1,256]{1,0:T(1,128)} %bitcast.13, s32[1,256]{1,0:T(1,128)} %cell.1, s32[1,256]{1,0:T(1,128)} %plane.1, ...), custom_call_target="tpu_custom_call" | custom-call | tf_op jit(solution)/shard_map/exchange/pallas_call | solution.py:227
  21.3 0.0 copy-start.4
  21.3 0.7 copy-done.4
  22.0 0.0 copy-start.6
  22.0 0.6 copy-done.6
  22.6 0.0 copy-start.9
  22.6 0.5 slice.3
  23.7 0.0 copy-start.10
  23.7 0.0 copy-start.11
  23.7 0.0 copy-start.12
  23.7 0.0 copy-start.13
  23.7 0.0 copy-start.14
  23.8 0.0 copy-start.15
  23.8 16.5 %grid_and_rows.2 = bf16[2048,256]{1,0:T(8,128)(2,1)} custom-call(s32[32,128]{1,0:T(8,128)} %copy-done.6, bf16[1024,128]{1,0:T(8,128)(2,1)} %copy-done.4, f32[4096,128]{1,0:T(8,128)S(1)} %get-tuple-element.107.table, bf16[4096,128]{1,0:T(8,128)(2,1)} %get-tuple-element.108.weight, bf16[256,256]{1,0:T(8,128)(2,1)} %constant.16.clone.over_r, ...), custom_call_target="tpu_custom_call" | custom-call | tf_op jit(solution)/shard_map/grid_and_rows/pallas_call | solution.py:325
  40.3 0.0 copy-done.9
  40.3 0.0 copy-done.10
  40.3 0.0 copy-done.11
  40.3 0.0 copy-done.12
  40.3 0.0 copy-done.13
  40.3 0.0 copy-done.14
  40.3 0.0 copy-done.15
  40.3 0.0 copy-start.1
  40.3 0.0 copy-start.5
  40.4 1.6 %copy-done.1 = bf16[2048,512]{1,0:T(8,128)(2,1)S(1)} copy-done((bf16[2048,512]{1,0:T(8,128)(2,1)S(1)}, bf16[2048,512]{1,0:T(8,128)(2,1)}, u32[]{:S(2)}) %copy-start.1) | copy-done | bytes 2097176
  41.9 0.0 copy-done.5
  41.9 34.5 %finish.1 = f32[64,128]{1,0:T(8,128)S(1)} custom-call(bf16[2048,256]{1,0:T(8,128)(2,1)} %get-tuple-element.239.pixels, bf16[128,64]{1,0:T(8,128)(2,1)S(1)} %copy-done.5, bf16[2048,512]{1,0:T(8,128)(2,1)S(1)} %copy-done.1), custom_call_target="tpu_custom_call" | custom-call | tf_op jit(solution)/shard_map/finish/pallas_call | solution.py:525
  76.5 0.1 reshape.14
  76.6 0.1 copy.10
  76.7 0.7 reshape.15
  (2 shorter events, 0.0 us)
Async XLA Ops:
  0.0 1.2 %copy-start.2 = (bf16[1,32,2,64,128]{4,3,2,1,0:T(8,128)(2,1)S(1)}, bf16[1,32,2,64,128]{4,3,2,1,0:T(8,128)(2,1)}, u32[]{:S(2)}) copy-start(bf16[1,32,2,64,128]{4,3,2,1,0:T(8,128)(2,1)} %param.14) | copy-start | bytes 3145732
  21.3 0.7 copy-start.4
  22.0 0.6 copy-start.6
  22.6 17.7 %copy-start.9 = (f32[4096,128]{1,0:T(8,128)}, f32[4096,128]{1,0:T(8,128)S(1)}, u32[]{:S(2)}) copy-start(f32[4096,128]{1,0:T(8,128)S(1)} %get-tuple-element.107.table) | copy-start | bytes 6291460
  23.7 16.6 %copy-start.10 = (bf16[4096,128]{1,0:T(8,128)(2,1)S(1)}, bf16[4096,128]{1,0:T(8,128)(2,1)}, u32[]{:S(2)}) copy-start(bf16[4096,128]{1,0:T(8,128)(2,1)} %constant.17.clone.over_x) | copy-start | bytes 3145732
  23.7 16.6 %copy-start.11 = (bf16[256,256]{1,0:T(8,128)(2,1)S(1)}, bf16[256,256]{1,0:T(8,128)(2,1)}, u32[]{:S(2)}) copy-start(bf16[256,256]{1,0:T(8,128)(2,1)} %constant.16.clone.over_r) | copy-start | bytes 393220
  23.7 16.6 %copy-start.12 = (f32[1,256,128]{2,1,0:T(8,128)S(1)}, f32[1,256,128]{2,1,0:T(8,128)}, u32[]{:S(2)}) copy-start(f32[1,256,128]{2,1,0:T(8,128)} %param.13) | copy-start | bytes 393220
  23.7 16.6 %copy-start.13 = (s32[1,256,1]{1,2,0:T(1,128)S(1)}, s32[1,256,1]{1,2,0:T(1,128)}, u32[]{:S(2)}) copy-start(s32[1,256,1]{1,2,0:T(1,128)} %param.15) | copy-start | bytes 3076
  23.7 16.6 %copy-start.14 = (s32[1,256]{1,0:T(1,128)S(1)}, s32[1,256]{1,0:T(1,128)}, u32[]{:S(2)}) copy-start(s32[1,256]{1,0:T(1,128)} %cell.1) | copy-start | bytes 3076
  23.8 16.6 %copy-start.15 = (s32[1,256]{1,0:T(1,128)S(1)}, s32[1,256]{1,0:T(1,128)}, u32[]{:S(2)}) copy-start(s32[1,256]{1,0:T(1,128)} %plane.1) | copy-start | bytes 3076
  40.3 1.6 %copy-start.1 = (bf16[2048,512]{1,0:T(8,128)(2,1)S(1)}, bf16[2048,512]{1,0:T(8,128)(2,1)}, u32[]{:S(2)}) copy-start(bf16[2048,512]{1,0:T(8,128)(2,1)} %constant.19.clone.over_v_hbm) | copy-start | bytes 6291460
  40.3 1.6 %copy-start.5 = (bf16[128,64]{1,0:T(8,128)(2,1)S(1)}, bf16[128,64]{1,0:T(8,128)(2,1)}, u32[]{:S(2)}) copy-start(bf16[128,64]{1,0:T(8,128)(2,1)} %constant.18.clone.over_t) | copy-start | bytes 49156

commit v3 on v2

--- a/solution.py
+++ b/solution.py
@@ -22,6 +22,8 @@
 HS = 129
 TOGETHER = 32
 WS = 65
+MS = 129
+ROWS = 80
 SLOTS = 32
 ALL = NT * SLOTS
 MIB = 1 << 20
@@ -52,15 +54,18 @@
 
 def column_tables():
     step = G // PIX - 1
-    m0 = np.arange(32)
-    angle = 2 * math.pi / 32 * ((step * (m0[:, None] - PIX // 2) * (m0[None, :] - 16)) % 32)
+    m0 = np.arange(64)
+    tile = np.arange(NT)
+    angle = 2 * math.pi / 64 * ((step * (m0[:, None] - PIX // 2) * (tile[None, :] - NT)) % 64)
     c, s = np.cos(angle), np.sin(angle)
     over_t = np.concatenate(split(np.block([[c, -s], [s, c]])), 0)
-    pixel = m0[:, None] + 32 * m0[None, :]
-    angle = 2 * math.pi / G * ((step * (pixel[:, :, None] - PIX // 2) * np.arange(256)) % G)
-    over_v = np.concatenate([np.cos(angle), -np.sin(angle)], 2) / G
-    high, low = split(over_v)
-    return over_t, np.concatenate([high, low], 1).reshape(32 * 64, 512)
+    pixel = m0[:, None] + 64 * np.arange(16)[None, :]
+    angle = 2 * math.pi / G * ((step * (pixel[:, :, None] - PIX // 2) * np.arange(128)) % G)
+    over_j = np.concatenate([np.cos(angle), -np.sin(angle)], 2) / G
+    high, low = split(over_j)
+    angle = 2 * math.pi / 64 * ((step * (m0[:, None] - PIX // 2) * (tile[None, :] + 1 - NT)) % 64)
+    lone = np.concatenate([np.cos(angle), np.sin(angle)], 0) / G
+    return over_t, np.concatenate([high, low], 1).reshape(64 * 32, 256), split(lone)[0]
 
 
 def iota(shape, axis):
@@ -77,8 +82,10 @@
 
 def fill_slots(samples, dest, cell, plane, skipped):
     column = jnp.bitwise_and(cell, 127)
-    owner = lax.shift_right_logical(column, 2)
-    inner = jnp.bitwise_and(column, 3)
+    mirror = lax.shift_right_logical(column, 6)
+    column = jnp.where(mirror == 1, 127 - column, column)
+    owner = lax.shift_right_logical(column, 1)
+    inner = jnp.bitwise_and(column, 1) + 2 * mirror
     row = dest * 4 + lax.shift_right_logical(cell, 7)
     named = iota((NT, BLK), 0) == owner
     one = jnp.where(named, 1.0, 0.0)
@@ -103,7 +110,7 @@
 
 def exchange_body(first, samples, dest, cell, plane, skipped, *rest):
     if first:
-        kern_hbm, recv, facts, table, weight, most, send, send_sem, recv_sem, kern, mine, seen, kern_sem, send_y, recv_y = rest
+        kern_hbm, recv, facts, table, weight, send, send_sem, recv_sem, kern, kern_sem = rest
     else:
         recv, facts, send, send_sem, recv_sem = rest
     me = lax.axis_index("tile")
@@ -120,13 +127,8 @@
         return 0
 
     lax.fori_loop(1, NT, greet, 0)
-    if first:
-        for i in range(1, NC):
-            pl.semaphore_signal(
-                barrier, inc=1, device_id=(me, lax.rem(chan + i, NC)), device_id_type=MESH
-            )
     send[...] = fill_slots(samples[...], dest[...], cell[...], plane[...], skipped[...])
-    pl.semaphore_wait(barrier, NT + NC - 2 if first else NT - 1)
+    pl.semaphore_wait(barrier, NT - 1)
 
     def copy(i):
         to = lax.rem(me + i, NT)
@@ -148,6 +150,7 @@
     recv[own, :] = send[own, :]
     if first:
         low = iota((S, 128), 1) < S
+        mirrored = jnp.where(iota((128, 128), 0) + iota((128, 128), 1) == 191, 1.0, 0.0).astype(BF)
 
         def prepare(w, _):
             base = pl.multiple_of(w * 128, 128)
@@ -157,12 +160,19 @@
             table[pl.ds(base, S), :] = turned
             swapped = pltpu.roll(turned, S, 1)
             table[pl.ds(base + S, S), :] = jnp.where(low, -swapped, swapped)
-            weight[pl.ds(base, S), :] = jnp.where(low, pltpu.roll(real, S, 1), imag).astype(BF)
-            weight[pl.ds(base + S, S), :] = jnp.where(low, -pltpu.roll(imag, S, 1), real).astype(BF)
+            for side in range(2):
+                at = base + side * NW * 128
+                weight[pl.ds(at, S), :] = jnp.where(low, pltpu.roll(real, S, 1), imag).astype(BF)
+                weight[pl.ds(at + S, S), :] = jnp.where(
+                    low, -pltpu.roll(imag, S, 1), real
+                ).astype(BF)
+                if side == 0:
+                    both = dot(kern[pl.ds(base, 128), :], mirrored)
+                    real, imag = both[:S], both[S:]
             return 0
 
         fetch.wait()
-        lax.fori_loop(0, 24, prepare, 0, unroll=2)
+        lax.fori_loop(0, NW, prepare, 0, unroll=2)
 
     def wait(i, _):
         copy(i).wait()
@@ -174,28 +184,6 @@
     lane = iota((NT, 128), 1)
     code = (pltpu.roll(raw, 64, 1) * 128.0 + raw) * 32.0 + pltpu.roll(raw, 96, 1)
     facts[...] = jnp.where(lane < SLOTS, code, raw).astype(jnp.int32)
-    if first:
-        largest = jnp.max(jnp.where(lane < 112, 0.0, raw), axis=0, keepdims=True)
-        largest = jnp.broadcast_to(jnp.max(largest, axis=1, keepdims=True), (8, 128))
-        mine[...] = largest
-
-        def tell(i):
-            return pltpu.make_async_remote_copy(
-                src_ref=mine,
-                dst_ref=seen.at[i],
-                send_sem=send_y.at[i],
-                recv_sem=recv_y.at[i],
-                device_id=(me, lax.rem(chan + i, NC)),
-                device_id_type=MESH,
-            )
-
-        for i in range(1, NC):
-            tell(i).start()
-        lax.fori_loop(24, NW, prepare, 0, unroll=2)
-        for i in range(1, NC):
-            tell(i).wait()
-            largest = jnp.maximum(largest, seen[i])
-        most[...] = largest
 
 
 def exchange(first, samples, dest, cell, plane, skipped, kern=None):
@@ -211,18 +199,13 @@
     if first:
         shapes += [
             jax.ShapeDtypeStruct((NW * 128, 128), F32),
-            jax.ShapeDtypeStruct((NW * 128, 128), BF),
-            jax.ShapeDtypeStruct((8, 128), F32),
+            jax.ShapeDtypeStruct((2 * NW * 128, 128), BF),
         ]
         operands.append(kern)
         specs.append(pl.BlockSpec(memory_space=pltpu.HBM))
         scratch += [
             pltpu.VMEM((NW * 128, 128), BF),
-            pltpu.VMEM((8, 128), F32),
-            pltpu.VMEM((NC, 8, 128), F32),
             pltpu.SemaphoreType.DMA,
-            pltpu.SemaphoreType.DMA((NC,)),
-            pltpu.SemaphoreType.DMA((NC,)),
         ]
     return pl.pallas_call(
         functools.partial(exchange_body, first),
@@ -231,7 +214,7 @@
         out_specs=[vmem] * len(shapes),
         scratch_shapes=scratch,
         compiler_params=pltpu.CompilerParams(
-            collective_id=0 if first else 2, has_side_effects=True, vmem_limit_bytes=32 * MIB
+            collective_id=0 if first else 2, has_side_effects=True, vmem_limit_bytes=60 * MIB
         ),
         name="exchange" if first else "exchange_more",
     )(*operands)
@@ -278,7 +261,8 @@
                 fill_a[pl.ds(i, 1), :] * table[pl.ds(base, S), :]
                 + fill_b[pl.ds(i, 1), :] * table[pl.ds(base + S, S), :]
             ).astype(BF)
-            patch = dot(left, weight[pl.ds(base, 128), :])
+            side = lax.shift_right_logical(fact, 13)
+            patch = dot(left, weight[pl.ds(pl.multiple_of(base + side * NW * 128, 128), 128), :])
             made.append((lax.shift_right_logical(fact, 5), patch))
         for place, patch in made:
             at = pl.ds(place * GS, S)
@@ -302,29 +286,46 @@
     pixels = grid
 
     def over_offsets(l0, _):
-        at = pl.multiple_of(l0 * HS, 1)
+        at = l0 * HS
         right = jnp.concatenate(
             [half[pl.ds(at, 128), :], half[pl.ds(128 * HS + at, 128), :]], axis=1
         ).astype(BF)
         got = dot(over_x[pl.ds(pl.multiple_of(l0 * 32, 32), 32), :], right)
         got = got[:16] + got[16:]
-        for side in range(2):
-            for q in range(2):
-                pixels[pl.ds(side * 2048 + 2 * l0 + q, 8, stride=256), :] = got[
-                    8 * q : 8 * q + 8, 128 * side : 128 * side + 128
-                ]
+        turned = pltpu.roll(got[:, 128:], 1, 1)
+        for q in range(2):
+            rows = slice(8 * q, 8 * q + 8)
+            pixels[pl.ds(2 * l0 + q, 8, stride=256), :] = got[rows, :128]
+            pixels[pl.ds(2048 + 2 * l0 + q, 8, stride=256), :] = (
+                turned[rows] if q == 0 else -turned[rows]
+            )
         return 0
 
     lax.fori_loop(0, 128, over_offsets, 0, unroll=16)
-    out[:, :128] = pixels[:2048, :].astype(out.dtype)
-    out[:, 128:] = pixels[2048:4096, :].astype(out.dtype)
-
-
-def grid_and_rows(facts, recv, table, weight, over_r, over_x, dtype):
+    lane = iota((1024, 128), 1)
+    place = jnp.bitwise_and(iota((1024, 128), 0), 31)
+    first = jnp.zeros((1024, 128), F32)
+    for q in range(2):
+        column = jnp.broadcast_to(pixels[pl.ds(2048 + q, 1024, stride=2), :][:, :1], (1024, 128))
+        first = jnp.where(lane == place + 32 * q, column, first)
+    by_owner = jnp.where(
+        lax.shift_right_logical(iota((NT * 16, 1024), 1), 5) * 16 == iota((NT * 16, 1024), 0), 1.0, 0.0
+    ).astype(BF)
+    lone = dot(by_owner, first.astype(BF)).astype(BF)
+    past = iota((64, 128), 1) > 0
+    for t in range(NT):
+        out[t * ROWS : t * ROWS + 64, :] = (
+            pixels[t * 64 : t * 64 + 64, :]
+            + jnp.where(past, pixels[2048 + t * 64 : 2048 + t * 64 + 64, :], 0.0)
+        ).astype(BF)
+        out[t * ROWS + 64 : t * ROWS + ROWS, :] = lone[t * 16 : t * 16 + 16]
+
+
+def grid_and_rows(facts, recv, table, weight, over_r, over_x):
     vmem = pl.BlockSpec(memory_space=pltpu.VMEM)
     return pl.pallas_call(
         grid_body,
-        out_shape=jax.ShapeDtypeStruct((2048, 256), dtype),
+        out_shape=jax.ShapeDtypeStruct((NT * ROWS, 128), BF),
         in_specs=[pl.BlockSpec(memory_space=pltpu.SMEM)] + [vmem] * 5,
         out_specs=vmem,
         scratch_shapes=[
@@ -339,24 +340,13 @@
     )(facts, recv, table, weight, over_r, over_x)
 
 
-def finish_body(
-    pixels,
-    over_t,
-    over_v_hbm,
-    out,
-    recv,
-    wide,
-    middle,
-    fold,
-    last,
-    over_v,
-    send_a,
-    recv_a,
-    send_b,
-    recv_b,
-    table_sem,
-):
-    fetch = pltpu.make_async_copy(over_v_hbm, over_v, table_sem)
+def finish_body(first, pixels, facts, over_t, lone_t, over_j_hbm, *rest):
+    if first:
+        out, most, *rest, mine, seen, send_y, recv_y = rest
+    else:
+        out, *rest = rest
+    recv, wide, middle, lone, fold, last, over_j, send_a, recv_a, send_b, recv_b, table_sem = rest
+    fetch = pltpu.make_async_copy(over_j_hbm, over_j, table_sem)
     fetch.start()
     me = lax.axis_index("tile")
     chan = lax.axis_index("chan")
@@ -382,13 +372,20 @@
         return 0
 
     lax.fori_loop(0, NT, greet_source, 0)
-    pl.semaphore_wait(barrier, jnp.where(stays, 2 * NT - 2, 2 * NT - 1))
+    greeted = 2 * NT - 1
+    if first:
+        greeted += NC - 1
+        for i in range(1, NC):
+            pl.semaphore_signal(
+                barrier, inc=1, device_id=(me, lax.rem(chan + i, NC)), device_id_type=MESH
+            )
+    pl.semaphore_wait(barrier, jnp.where(stays, greeted - 1, greeted))
 
     def copy(i):
         to = lax.rem(me + i, NT)
         return pltpu.make_async_remote_copy(
-            src_ref=pixels.at[pl.ds(pl.multiple_of(to * 64, 64), 64)],
-            dst_ref=recv.at[pl.ds(pl.multiple_of(me * 64, 64), 64)],
+            src_ref=pixels.at[pl.ds(pl.multiple_of(to * ROWS, 16), ROWS)],
+            dst_ref=recv.at[pl.ds(pl.multiple_of(me * ROWS, 16), ROWS)],
             send_sem=send_a.at[i],
             recv_sem=recv_a.at[i],
             device_id=(to, chan),
@@ -400,7 +397,24 @@
         return 0
 
     lax.fori_loop(1, NT, start, 0)
-    own = pl.ds(pl.multiple_of(me * 64, 64), 64)
+    if first:
+        known = jnp.where(iota((NT, 128), 1) < 112, 0, facts[...]).astype(F32)
+        known = jnp.max(jnp.max(known, axis=0, keepdims=True), axis=1, keepdims=True)
+        mine[...] = jnp.broadcast_to(known, (8, 128))
+
+        def tell(i):
+            return pltpu.make_async_remote_copy(
+                src_ref=mine,
+                dst_ref=seen.at[i],
+                send_sem=send_y.at[i],
+                recv_sem=recv_y.at[i],
+                device_id=(me, lax.rem(chan + i, NC)),
+                device_id_type=MESH,
+            )
+
+        for i in range(1, NC):
+            tell(i).start()
+    own = pl.ds(pl.multiple_of(me * ROWS, 16), ROWS)
     recv[own, :] = pixels[own, :]
 
     def wait(i, _):
@@ -410,51 +424,42 @@
     lax.fori_loop(1, NT, wait, 0)
 
     def widen(t, _):
-        block = recv[pl.ds(pl.multiple_of(t * 64, 64), 64), :].astype(F32)
-        wide[pl.ds(t * WS, 64), :] = block[:, :128]
-        wide[pl.ds((NT + t) * WS, 64), :] = block[:, 128:]
+        block = recv[pl.ds(pl.multiple_of(t * ROWS, 16), ROWS), :].astype(F32)
+        wide[pl.ds(t * WS, 64), :] = block[:64]
+        lone[pl.ds(t, 1), :] = block[64:65]
         return 0
 
     lax.fori_loop(0, NT, widen, 0, unroll=4)
 
     def over_tiles(l, _):
-        rows = [
-            jnp.concatenate(
-                [wide[pl.ds(side * NT * WS + 2 * l + q, NT, stride=WS), :] for side in range(2)],
-                axis=1,
-            )
-            for q in range(2)
-        ]
+        rows = [wide[pl.ds(2 * l + q, NT, stride=WS), :] for q in range(2)]
         got = dot(over_t[...], jnp.concatenate(rows, axis=0).astype(BF))
-        got = got[:64] + got[64:]
-        middle[pl.ds(l * WS, 64), :] = got[:, :128]
-        middle[pl.ds((32 + l) * WS, 64), :] = got[:, 128:]
+        middle[pl.ds(l * MS, 128), :] = got[:128] + got[128:]
         return 0
 
     lax.fori_loop(0, 32, over_tiles, 0, unroll=8)
     fetch.wait()
+    alone = dot(lone_t[...], lone[...].astype(BF))
+    wide[0:64, :] = alone[:64] - pltpu.roll(alone[64:], 96, 1)
 
     def over_columns(a, _):
-        made = []
-        for b in range(4):
-            m0 = b * 8 + a
-            right = jnp.concatenate(
-                [
-                    middle[pl.ds(side * 32 * WS + 32 * q + m0, 32, stride=WS), :]
-                    for q in range(2)
-                    for side in range(2)
-                ],
-                axis=1,
-            )
-            high = right.astype(BF)
-            low = (right - high.astype(F32)).astype(BF)
-            left = over_v[pl.ds(pl.multiple_of(m0 * 64, 64), 64), :]
-            got = dot_t(left, high)
-            made.append(got[:32] + got[32:] + dot_t(left[:32], low))
-        fold[pl.ds(a, 32, stride=8), :] = jnp.concatenate(made, axis=1)
-        return 0
-
-    lax.fori_loop(0, 8, over_columns, 0, unroll=4)
+        for h in range(2):
+            made = []
+            for b in range(4):
+                m0 = h * 32 + b * 8 + a
+                right = jnp.concatenate(
+                    [middle[pl.ds(64 * q + m0, 32, stride=MS), :] for q in range(2)], axis=1
+                )
+                high = right.astype(BF)
+                low = (right - high.astype(F32)).astype(BF)
+                left = over_j[pl.ds(pl.multiple_of(m0 * 32, 32), 32), :]
+                got = dot_t(left, high)
+                got = got[:16] + got[16:] + dot_t(left[:16], low)
+                made.append(got + wide[pl.ds(m0, 1), :][:, :32])
+            fold[pl.ds(h * 8 + a, 16, stride=16), :] = jnp.concatenate(made, axis=1)
+        return 0
+
+    lax.fori_loop(0, 8, over_columns, 0, unroll=2)
     slot = lax.rem(me, 8) * NC + chan
 
     def give(i):
@@ -494,6 +499,11 @@
         return 0
 
     lax.fori_loop(1, NT, start_b, 0)
+    if first:
+        for i in range(1, NC):
+            tell(i).wait()
+            known = jnp.maximum(known, jnp.max(seen[i][:1], axis=1, keepdims=True))
+        most[0, 0] = jnp.max(known)
 
     def wait_b(i, _):
         @pl.when(jnp.logical_or(jnp.logical_not(stays), i != slot))
@@ -503,80 +513,89 @@
         return 0
 
     lax.fori_loop(0, NT, wait_b, 0)
-
-    @pl.when(jnp.logical_not(stays))
-    def _():
-        give(0).wait_send()
-
-    def sent_b(i, _):
-        give(i).wait_send()
-        return 0
-
-    lax.fori_loop(1, NT, sent_b, 0)
     for t in range(8):
         total = last[t * 32 : t * 32 + 8, :]
         for c in range(1, NC):
             total = total + last[t * 32 + c * 8 : t * 32 + c * 8 + 8, :]
         out[t * 8 : t * 8 + 8, :] = total
 
-
-def finish(pixels, over_t, over_v):
+    @pl.when(jnp.logical_not(stays))
+    def _():
+        give(0).wait_send()
+
+    def sent_b(i, _):
+        give(i).wait_send()
+        return 0
+
+    lax.fori_loop(1, NT, sent_b, 0)
+
+
+def finish(first, pixels, facts, over_t, lone_t, over_j):
     vmem = pl.BlockSpec(memory_space=pltpu.VMEM)
+    shapes, outs = [jax.ShapeDtypeStruct((64, 128), F32)], [vmem]
+    scratch = [
+        pltpu.VMEM((NT * ROWS, 128), BF),
+        pltpu.VMEM((NT * WS, 128), F32),
+        pltpu.VMEM((32 * MS, 128), F32),
+        pltpu.VMEM((NT, 128), F32),
+        pltpu.VMEM((256, 128), F32),
+        pltpu.VMEM((256, 128), F32),
+        pltpu.VMEM((2048, 256), BF),
+        pltpu.SemaphoreType.DMA((NT,)),
+        pltpu.SemaphoreType.DMA((NT,)),
+        pltpu.SemaphoreType.DMA((NT,)),
+        pltpu.SemaphoreType.DMA((NT,)),
+        pltpu.SemaphoreType.DMA,
+    ]
+    if first:
+        shapes.append(jax.ShapeDtypeStruct((1, 1), F32))
+        outs.append(pl.BlockSpec(memory_space=pltpu.SMEM))
+        scratch += [
+            pltpu.VMEM((8, 128), F32),
+            pltpu.VMEM((NC, 8, 128), F32),
+            pltpu.SemaphoreType.DMA((NC,)),
+            pltpu.SemaphoreType.DMA((NC,)),
+        ]
     return pl.pallas_call(
-        finish_body,
-        out_shape=jax.ShapeDtypeStruct((64, 128), F32),
-        in_specs=[vmem] * 2 + [pl.BlockSpec(memory_space=pltpu.HBM)],
-        out_specs=vmem,
-        scratch_shapes=[
-            pltpu.VMEM((2048, 256), BF),
-            pltpu.VMEM((2 * NT * WS, 128), F32),
-            pltpu.VMEM((2 * 32 * WS, 128), F32),
-            pltpu.VMEM((256, 128), F32),
-            pltpu.VMEM((256, 128), F32),
-            pltpu.VMEM((2048, 512), BF),
-            pltpu.SemaphoreType.DMA((NT,)),
-            pltpu.SemaphoreType.DMA((NT,)),
-            pltpu.SemaphoreType.DMA((NT,)),
-            pltpu.SemaphoreType.DMA((NT,)),
-            pltpu.SemaphoreType.DMA,
-        ],
+        functools.partial(finish_body, first),
+        out_shape=shapes,
+        in_specs=[vmem] * 4 + [pl.BlockSpec(memory_space=pltpu.HBM)],
+        out_specs=outs,
+        scratch_shapes=scratch,
         compiler_params=pltpu.CompilerParams(
-            collective_id=1, has_side_effects=True, vmem_limit_bytes=32 * MIB
+            collective_id=1 if first else 3, has_side_effects=True, vmem_limit_bytes=60 * MIB
         ),
-        name="finish",
-    )(pixels, over_t, over_v)
+        name="finish" if first else "finish_more",
+    )(pixels, facts, over_t, lone_t, over_j)
 
 
 def local(visibilities, kernels, destination, cell, plane):
     over_r, over_x = (jnp.asarray(t) for t in row_tables())
-    over_t, over_v = (jnp.asarray(t) for t in column_tables())
+    over_t, over_j, lone_t = (jnp.asarray(t) for t in column_tables())
     samples = visibilities[0]
     dest = destination.reshape(1, BLK)
     kern = kernels.reshape(NW * 128, 128)
     none = jnp.zeros((1, BLK), jnp.int32)
-    recv, facts, table, weight, most = exchange(True, samples, dest, cell, plane, none, kern)
-    largest = most[0, 0]
-    pixels = grid_and_rows(facts, recv, table, weight, over_r, over_x, BF)
-
-    def more(pixels):
+    recv, facts, table, weight = exchange(True, samples, dest, cell, plane, none, kern)
+    pixels = grid_and_rows(facts, recv, table, weight, over_r, over_x)
+    image, most = finish(True, pixels, facts, over_t, lone_t, over_j)
+    most = most[0, 0]
+
+    def more(image):
         def again(state):
             done, total = state
-            more_recv, more_facts = exchange(
-                False, samples, dest, cell, plane, jnp.broadcast_to(done, (1, BLK))
-            )
-            return done + CAP, total + grid_and_rows(
-                more_facts, more_recv, table, weight, over_r, over_x, F32
-            )
+            skipped = jnp.broadcast_to(done, (1, BLK))
+            recv, facts = exchange(False, samples, dest, cell, plane, skipped)
+            pixels = grid_and_rows(facts, recv, table, weight, over_r, over_x)
+            [terms] = finish(False, pixels, facts, over_t, lone_t, over_j)
+            return done + CAP, total + terms
 
         return lax.while_loop(
-            lambda state: state[0].astype(F32) < largest,
-            again,
-            (jnp.int32(CAP), pixels.astype(F32)),
-        )[1].astype(BF)
-
-    pixels = lax.cond(largest > CAP, more, lambda p: p, pixels)
-    out = finish(pixels, over_t, over_v)
-    return out.reshape(8, 8, 4, 32).transpose(0, 3, 2, 1).reshape(256, 32)
+            lambda state: state[0].astype(F32) < most, again, (jnp.int32(CAP), image)
+        )[1]
+
+    image = lax.cond(most > CAP, more, lambda terms: terms, image)
+    return image.reshape(8, 8, 4, 32).transpose(0, 3, 2, 1).reshape(256, 32)
 
 
 def solution(mesh):

time: 77.9 us -> 66.2 us (0.85)
  Pallas kernels: 71.1 us -> 63.8 us
  local copies, waits for them, and re-layouts: 5.53 us -> 1.52 us
    unnamed x24 -> x16, local copies, waits for them, and re-layouts: 4.12 us -> 0.05 us
    pallas_call x1, Pallas kernels: 20.1 us -> 16.1 us  [exchange(): pl.pallas_call(functools.partial(exchange_body, first), out_shape=shapes,...]
    pallas_call x2, Pallas kernels: 51 us -> 47.7 us  [the longest x1 29 us: finish(): pl.pallas_call(functools.partial(finish_body, first), out_shape=shapes, i...]
where the time goes in v3:
time: 66.2 us; the launch traced here: 66.1 us
  Pallas kernels  63.8 us (96%)
  local copies, waits for them, and re-layouts  1.52 us (2%)
  between operations  0.71 us (1%)
    pallas_call x1, Pallas kernels, finish(): pl.pallas_call(functools.partial(finish_body, first), out_shape=shapes, i...  29 us
    pallas_call x1, Pallas kernels, grid_and_rows(): pl.pallas_call(grid_body, out_shape=jax.ShapeDtypeStruct((NT * ROWS, 128)...  18.7 us
    pallas_call x1, Pallas kernels, exchange(): pl.pallas_call(functools.partial(exchange_body, first), out_shape=shapes,...  16.1 us

profile of v3, /device:TPU:1, one launch (start us, length us, event | category | flops | bytes accessed | tf_op | source)
XLA Modules:
  0.0 66.1 jit_solution(9668673583588704733)
XLA Ops:
  0.0 0.6 broadcast_in_dim.6.skipped
  0.6 16.1 %exchange.1 = (bf16[1024,128]{1,0:T(8,128)(2,1)}, s32[32,128]{1,0:T(8,128)}, f32[4096,128]{1,0:T(8,128)S(1)}, bf16[8192,128]{1,0:T(8,128)(2,1)}) custom-call(f32[256,128]{1,0:T(8,128)} %bitcast.11, s32[1,256]{1,0:T(1,128)} %bitcast.15, s32[1,256]{1,0:T(1,128)} %cell.1, s32[1,256]{1,0:T(1,128)} %plane.1, s32[1,256]{1,0:T(1,128)} %broadcast_in_dim.6.skipped, ...), custom_call_target="tpu_custom_call" | custom-call | tf_op jit(solution)/shard_map/exchange/pallas_call | solution.py:210
  16.7 0.0 copy-start
  16.7 0.0 copy-start.3
  16.7 0.0 copy-start.4
  16.7 0.0 copy-start.1
  16.7 0.0 copy-start.2
  16.8 0.0 copy-start.5
  16.8 0.0 copy-start.6
  16.8 0.0 copy-start.7
  16.8 18.7 %grid_and_rows.2.pixels = bf16[2560,128]{1,0:T(8,128)(2,1)} custom-call(s32[32,128]{1,0:T(8,128)} %get-tuple-element.129.facts, bf16[1024,128]{1,0:T(8,128)(2,1)} %get-tuple-element.130.recv, f32[4096,128]{1,0:T(8,128)S(1)} %get-tuple-element.131.table, bf16[8192,128]{1,0:T(8,128)(2,1)} %get-tuple-element.132.weight, ...), custom_call_target="tpu_custom_call" | custom-call | tf_op jit(solution)/shard_map/grid_and_rows/pallas_call | solution.py:326
  35.5 0.0 copy-done
  35.5 0.0 copy-done.3
  35.5 0.0 copy-done.4
  35.5 29.0 %finish.1 = (f32[64,128]{1,0:T(8,128)S(1)}, f32[1,1]{1,0:T(1,128)}) custom-call(bf16[2560,128]{1,0:T(8,128)(2,1)} %grid_and_rows.2.pixels, s32[32,128]{1,0:T(8,128)} %get-tuple-element.129.facts, bf16[256,64]{1,0:T(8,128)(2,1)S(1)} %copy-done.3, bf16[128,32]{1,0:T(8,128)(2,1)S(1)} %copy-done.4, bf16[2048,256]{1,0:T(8,128)(2,1)S(1)} %copy-done), custom_call_target="tpu_custom_call" | custom-call | tf_op jit(solution)/shard_map/finish/pallas_call | solution.py:559
  65.1 0.0 copy-done.1
  65.1 0.0 copy-done.2
  65.1 0.0 copy-done.5
  65.1 0.0 copy-done.6
  65.1 0.0 copy-done.7
  65.1 0.1 reshape.14
  65.3 0.1 copy.13
  65.4 0.7 %reshape.15 = f32[256,32]{0,1:T(8,128)} reshape(f32[8,32,4,8]{1,0,3,2:T(8,128)S(1)} %bitcast.14) | data formatting | bytes 65536 | tf_op jit(solution)/shard_map/reshape | solution.py:598
  (1 shorter events, 0.0 us)
Async XLA Ops:
  16.7 18.8 %copy-start = (bf16[2048,256]{1,0:T(8,128)(2,1)S(1)}, bf16[2048,256]{1,0:T(8,128)(2,1)}, u32[]{:S(2)}) copy-start(bf16[2048,256]{1,0:T(8,128)(2,1)} %constant.21.clone.over_j_hbm) | copy-start | bytes 3145732
  16.7 18.8 %copy-start.3 = (bf16[256,64]{1,0:T(8,128)(2,1)S(1)}, bf16[256,64]{1,0:T(8,128)(2,1)}, u32[]{:S(2)}) copy-start(bf16[256,64]{1,0:T(8,128)(2,1)} %constant.20.clone.over_t) | copy-start | bytes 98308
  16.7 18.8 %copy-start.4 = (bf16[128,32]{1,0:T(8,128)(2,1)S(1)}, bf16[128,32]{1,0:T(8,128)(2,1)}, u32[]{:S(2)}) copy-start(bf16[128,32]{1,0:T(8,128)(2,1)} %constant.22.clone.lone_t) | copy-start | bytes 24580
  16.7 48.3 %copy-start.1 = (bf16[256,256]{1,0:T(8,128)(2,1)S(1)}, bf16[256,256]{1,0:T(8,128)(2,1)}, u32[]{:S(2)}) copy-start(bf16[256,256]{1,0:T(8,128)(2,1)} %constant.18.clone.over_r) | copy-start | bytes 393220
  16.7 48.3 %copy-start.2 = (f32[1,256,128]{2,1,0:T(8,128)S(1)}, f32[1,256,128]{2,1,0:T(8,128)}, u32[]{:S(2)}) copy-start(f32[1,256,128]{2,1,0:T(8,128)} %param.14) | copy-start | bytes 393220
  16.8 48.3 %copy-start.5 = (s32[1,256,1]{1,2,0:T(1,128)S(1)}, s32[1,256,1]{1,2,0:T(1,128)}, u32[]{:S(2)}) copy-start(s32[1,256,1]{1,2,0:T(1,128)} %param.16) | copy-start | bytes 3076
  16.8 48.3 %copy-start.6 = (s32[1,256]{1,0:T(1,128)S(1)}, s32[1,256]{1,0:T(1,128)}, u32[]{:S(2)}) copy-start(s32[1,256]{1,0:T(1,128)} %cell.1) | copy-start | bytes 3076
  16.8 48.3 %copy-start.7 = (s32[1,256]{1,0:T(1,128)S(1)}, s32[1,256]{1,0:T(1,128)}, u32[]{:S(2)}) copy-start(s32[1,256]{1,0:T(1,128)} %plane.1) | copy-start | bytes 3076

commit v4 on v3

--- a/solution.py
+++ b/solution.py
@@ -30,6 +30,7 @@
 BF = jnp.bfloat16
 F32 = jnp.float32
 MESH = pl.DeviceIdType.MESH
+HALF = jax.ShapeDtypeStruct((2 * 128 * HS, 128), F32)
 
 
 def split(table):
@@ -108,11 +109,11 @@
     return slots.astype(BF)
 
 
-def exchange_body(first, samples, dest, cell, plane, skipped, *rest):
+def exchange_body(first, samples, dest, cell, plane, *rest):
     if first:
         kern_hbm, recv, facts, table, weight, send, send_sem, recv_sem, kern, kern_sem = rest
     else:
-        recv, facts, send, send_sem, recv_sem = rest
+        skipped, recv, facts, send, send_sem, recv_sem = rest
     me = lax.axis_index("tile")
     chan = lax.axis_index("chan")
     barrier = pltpu.get_barrier_semaphore()
@@ -127,7 +128,7 @@
         return 0
 
     lax.fori_loop(1, NT, greet, 0)
-    send[...] = fill_slots(samples[...], dest[...], cell[...], plane[...], skipped[...])
+    send[...] = fill_slots(samples[...], dest[...], cell[...], plane[...], 0 if first else skipped[...])
     pl.semaphore_wait(barrier, NT - 1)
 
     def copy(i):
@@ -186,11 +187,11 @@
     facts[...] = jnp.where(lane < SLOTS, code, raw).astype(jnp.int32)
 
 
-def exchange(first, samples, dest, cell, plane, skipped, kern=None):
+def exchange(first, samples, dest, cell, plane, last):
     vmem = pl.BlockSpec(memory_space=pltpu.VMEM)
     shapes = [jax.ShapeDtypeStruct((ALL, 128), BF), jax.ShapeDtypeStruct((NT, 128), jnp.int32)]
-    operands = [samples, dest, cell, plane, skipped]
-    specs = [vmem] * 5
+    operands = [samples, dest, cell, plane, last]
+    specs = [vmem] * 4 + [pl.BlockSpec(memory_space=pltpu.HBM) if first else vmem]
     scratch = [
         pltpu.VMEM((ALL, 128), BF),
         pltpu.SemaphoreType.DMA((NT,)),
@@ -201,8 +202,6 @@
             jax.ShapeDtypeStruct((NW * 128, 128), F32),
             jax.ShapeDtypeStruct((2 * NW * 128, 128), BF),
         ]
-        operands.append(kern)
-        specs.append(pl.BlockSpec(memory_space=pltpu.HBM))
         scratch += [
             pltpu.VMEM((NW * 128, 128), BF),
             pltpu.SemaphoreType.DMA,
@@ -214,13 +213,13 @@
         out_specs=[vmem] * len(shapes),
         scratch_shapes=scratch,
         compiler_params=pltpu.CompilerParams(
-            collective_id=0 if first else 2, has_side_effects=True, vmem_limit_bytes=60 * MIB
+            collective_id=0 if first else 2, has_side_effects=True, vmem_limit_bytes=40 * MIB
         ),
         name="exchange" if first else "exchange_more",
     )(*operands)
 
 
-def grid_body(facts, recv, table, weight, over_r, over_x, out, grid, half, fill_a, fill_b, todo):
+def grid_body(facts, recv, table, weight, over_r, half, grid, fill_a, fill_b, todo):
     lane = iota((ALL, 128), 1)
     slot = iota((ALL, 128), 0)
     blocks = jnp.where(jnp.bitwise_and(slot, SLOTS - 1) == CAP, 0.0, recv[...].astype(F32))
@@ -228,23 +227,12 @@
     fill_a[...] = jnp.where(lane < S, blocks, swapped)
     fill_b[...] = jnp.where(lane < S, swapped, blocks)
 
-    def clear(i, _):
-        grid[pl.ds(pl.multiple_of(i * 512, 512), 512), :] = jnp.zeros((512, 128), F32)
-        return 0
-
-    lax.fori_loop(0, GS, clear, 0)
-
     def from_source(t, at):
-        number = facts[t, 96]
-
-        def eight(j, _):
-            for k in range(8):
-                i = j * 8 + k
-                todo[at + i] = facts[t, i] * ALL + t * SLOTS + i
-            return 0
-
-        lax.fori_loop(0, lax.shift_right_logical(number + 7, 3), eight, 0)
-        return at + number
+        part = grid.shape[0] // NT
+        grid[pl.ds(pl.multiple_of(t * part, 8), part), :] = jnp.zeros((part, 128), F32)
+        for i in range(SLOTS):
+            todo[at + i] = facts[t, i] * ALL + t * SLOTS + i
+        return at + facts[t, 96]
 
     number = lax.fori_loop(0, NT, from_source, 0)
     for k in range(TOGETHER):
@@ -283,9 +271,86 @@
         return 0
 
     lax.fori_loop(0, S, over_rows, 0, unroll=8)
-    pixels = grid
-
-    def over_offsets(l0, _):
+
+
+def grid_and_rows(facts, recv, table, weight, over_r):
+    vmem = pl.BlockSpec(memory_space=pltpu.VMEM)
+    return pl.pallas_call(
+        grid_body,
+        out_shape=HALF,
+        in_specs=[pl.BlockSpec(memory_space=pltpu.SMEM)] + [vmem] * 4,
+        out_specs=vmem,
+        scratch_shapes=[
+            pltpu.VMEM((512 * GS, 128), F32),
+            pltpu.VMEM((ALL, 128), F32),
+            pltpu.VMEM((ALL, 128), F32),
+            pltpu.SMEM((ALL + 64,), jnp.int32),
+        ],
+        compiler_params=pltpu.CompilerParams(vmem_limit_bytes=24 * MIB),
+        name="grid_and_rows",
+    )(facts, recv, table, weight, over_r)
+
+
+def finish_body(first, half, facts, over_x, over_t, lone_t, over_j, *rest):
+    if first:
+        out, most, *rest, mine, seen, send_y, recv_y = rest
+    else:
+        out, *rest = rest
+    pixels, send, recv, wide, middle, lone, fold, last, send_a, recv_a, send_b, recv_b = rest
+    me = lax.axis_index("tile")
+    chan = lax.axis_index("chan")
+    home = me // 8
+    stays = home == chan
+    barrier = pltpu.get_barrier_semaphore()
+
+    def greet(i, _):
+        pl.semaphore_signal(
+            barrier, inc=1, device_id=(lax.rem(me + i, NT), chan), device_id_type=MESH
+        )
+        return 0
+
+    lax.fori_loop(1, NT, greet, 0)
+
+    def greet_source(i, _):
+        from_t, from_c = chan * 8 + i // NC, lax.rem(i, NC)
+
+        @pl.when(jnp.logical_or(from_t != me, from_c != chan))
+        def _():
+            pl.semaphore_signal(barrier, inc=1, device_id=(from_t, from_c), device_id_type=MESH)
+
+        return 0
+
+    lax.fori_loop(0, NT, greet_source, 0)
+    greeted = 2 * NT - 1
+    if first:
+        greeted += NC - 1
+        for i in range(1, NC):
+            pl.semaphore_signal(
+                barrier, inc=1, device_id=(me, lax.rem(chan + i, NC)), device_id_type=MESH
+            )
+
+    def give_rows(to):
+        return pltpu.make_async_remote_copy(
+            src_ref=send.at[pl.ds(pl.multiple_of(to * ROWS, 16), ROWS)],
+            dst_ref=recv.at[pl.ds(pl.multiple_of(me * ROWS, 16), ROWS)],
+            send_sem=send_a.at[to],
+            recv_sem=recv_a.at[me],
+            device_id=(to, chan),
+            device_id_type=MESH,
+        )
+
+    def take_rows(source):
+        at = pl.ds(pl.multiple_of(source * ROWS, 16), ROWS)
+        return pltpu.make_async_remote_copy(
+            src_ref=recv.at[at],
+            dst_ref=recv.at[at],
+            send_sem=send_a.at[source],
+            recv_sem=recv_a.at[source],
+            device_id=(source, chan),
+            device_id_type=MESH,
+        )
+
+    def over_offsets(l0):
         at = l0 * HS
         right = jnp.concatenate(
             [half[pl.ds(at, 128), :], half[pl.ds(128 * HS + at, 128), :]], axis=1
@@ -299,104 +364,51 @@
             pixels[pl.ds(2048 + 2 * l0 + q, 8, stride=256), :] = (
                 turned[rows] if q == 0 else -turned[rows]
             )
-        return 0
-
-    lax.fori_loop(0, 128, over_offsets, 0, unroll=16)
-    lane = iota((1024, 128), 1)
-    place = jnp.bitwise_and(iota((1024, 128), 0), 31)
-    first = jnp.zeros((1024, 128), F32)
-    for q in range(2):
-        column = jnp.broadcast_to(pixels[pl.ds(2048 + q, 1024, stride=2), :][:, :1], (1024, 128))
-        first = jnp.where(lane == place + 32 * q, column, first)
-    by_owner = jnp.where(
-        lax.shift_right_logical(iota((NT * 16, 1024), 1), 5) * 16 == iota((NT * 16, 1024), 0), 1.0, 0.0
-    ).astype(BF)
-    lone = dot(by_owner, first.astype(BF)).astype(BF)
+
     past = iota((64, 128), 1) > 0
-    for t in range(NT):
-        out[t * ROWS : t * ROWS + 64, :] = (
-            pixels[t * 64 : t * 64 + 64, :]
-            + jnp.where(past, pixels[2048 + t * 64 : 2048 + t * 64 + 64, :], 0.0)
+    lane = iota((32, 128), 1)
+    place = iota((32, 128), 0)
+
+    def pack(i, part):
+        to = jnp.bitwise_and(i + me // 4, 7) * 4 + part
+        rows = pl.multiple_of(to * 64, 64)
+        mirror = pixels[pl.ds(2048 + rows, 64), :]
+        at = pl.multiple_of(to * ROWS, 16)
+        send[pl.ds(at, 64), :] = (
+            pixels[pl.ds(rows, 64), :] + jnp.where(past, mirror, 0.0)
         ).astype(BF)
-        out[t * ROWS + 64 : t * ROWS + ROWS, :] = lone[t * 16 : t * 16 + 16]
-
-
-def grid_and_rows(facts, recv, table, weight, over_r, over_x):
-    vmem = pl.BlockSpec(memory_space=pltpu.VMEM)
-    return pl.pallas_call(
-        grid_body,
-        out_shape=jax.ShapeDtypeStruct((NT * ROWS, 128), BF),
-        in_specs=[pl.BlockSpec(memory_space=pltpu.SMEM)] + [vmem] * 5,
-        out_specs=vmem,
-        scratch_shapes=[
-            pltpu.VMEM((512 * GS, 128), F32),
-            pltpu.VMEM((2 * 128 * HS, 128), F32),
-            pltpu.VMEM((ALL, 128), F32),
-            pltpu.VMEM((ALL, 128), F32),
-            pltpu.SMEM((ALL + 64,), jnp.int32),
-        ],
-        compiler_params=pltpu.CompilerParams(vmem_limit_bytes=56 * MIB),
-        name="grid_and_rows",
-    )(facts, recv, table, weight, over_r, over_x)
-
-
-def finish_body(first, pixels, facts, over_t, lone_t, over_j_hbm, *rest):
-    if first:
-        out, most, *rest, mine, seen, send_y, recv_y = rest
-    else:
-        out, *rest = rest
-    recv, wide, middle, lone, fold, last, over_j, send_a, recv_a, send_b, recv_b, table_sem = rest
-    fetch = pltpu.make_async_copy(over_j_hbm, over_j, table_sem)
-    fetch.start()
-    me = lax.axis_index("tile")
-    chan = lax.axis_index("chan")
-    home = me // 8
-    stays = home == chan
-    barrier = pltpu.get_barrier_semaphore()
-
-    def greet(i, _):
-        pl.semaphore_signal(
-            barrier, inc=1, device_id=(lax.rem(me + i, NT), chan), device_id_type=MESH
-        )
-        return 0
-
-    lax.fori_loop(1, NT, greet, 0)
-
-    def greet_source(i, _):
-        from_t, from_c = chan * 8 + i // NC, lax.rem(i, NC)
-
-        @pl.when(jnp.logical_or(from_t != me, from_c != chan))
+        spread = jnp.zeros((32, 128), F32)
+        for q in range(2):
+            column = pixels[pl.ds(2048 + rows + q, 32, stride=2), :][:, :1]
+            spread = jnp.where(
+                lane == place + 32 * q, jnp.broadcast_to(column, (32, 128)), spread
+            )
+        spread = jnp.sum(spread, axis=0, keepdims=True)
+        send[pl.ds(at + 64, 16), :] = jnp.broadcast_to(spread, (16, 128)).astype(BF)
+        return part
+
+    def start(i, part):
+        to = jnp.bitwise_and(i + me // 4, 7) * 4 + part
+
+        @pl.when(to != me)
         def _():
-            pl.semaphore_signal(barrier, inc=1, device_id=(from_t, from_c), device_id_type=MESH)
-
-        return 0
-
-    lax.fori_loop(0, NT, greet_source, 0)
-    greeted = 2 * NT - 1
-    if first:
-        greeted += NC - 1
-        for i in range(1, NC):
-            pl.semaphore_signal(
-                barrier, inc=1, device_id=(me, lax.rem(chan + i, NC)), device_id_type=MESH
-            )
-    pl.semaphore_wait(barrier, jnp.where(stays, greeted - 1, greeted))
-
-    def copy(i):
-        to = lax.rem(me + i, NT)
-        return pltpu.make_async_remote_copy(
-            src_ref=pixels.at[pl.ds(pl.multiple_of(to * ROWS, 16), ROWS)],
-            dst_ref=recv.at[pl.ds(pl.multiple_of(me * ROWS, 16), ROWS)],
-            send_sem=send_a.at[i],
-            recv_sem=recv_a.at[i],
-            device_id=(to, chan),
-            device_id_type=MESH,
-        )
-
-    def start(i, _):
-        copy(i).start()
-        return 0
-
-    lax.fori_loop(1, NT, start, 0)
+            give_rows(to).start()
+
+        return part
+
+    for turn in range(4):
+        part = jnp.bitwise_and(me + turn, 3)
+
+        def some(j, part):
+            for k in range(16):
+                over_offsets(part * 32 + j * 16 + k)
+            return part
+
+        lax.fori_loop(0, 2, some, part)
+        lax.fori_loop(0, 8, pack, part, unroll=2)
+        if turn == 0:
+            pl.semaphore_wait(barrier, jnp.where(stays, greeted - 1, greeted))
+        lax.fori_loop(0, 8, start, part)
     if first:
         known = jnp.where(iota((NT, 128), 1) < 112, 0, facts[...]).astype(F32)
         known = jnp.max(jnp.max(known, axis=0, keepdims=True), axis=1, keepdims=True)
@@ -415,10 +427,10 @@
         for i in range(1, NC):
             tell(i).start()
     own = pl.ds(pl.multiple_of(me * ROWS, 16), ROWS)
-    recv[own, :] = pixels[own, :]
+    recv[own, :] = send[own, :]
 
     def wait(i, _):
-        copy(i).wait()
+        take_rows(lax.rem(me + i, NT)).wait_recv()
         return 0
 
     lax.fori_loop(1, NT, wait, 0)
@@ -438,7 +450,6 @@
         return 0
 
     lax.fori_loop(0, 32, over_tiles, 0, unroll=8)
-    fetch.wait()
     alone = dot(lone_t[...], lone[...].astype(BF))
     wide[0:64, :] = alone[:64] - pltpu.roll(alone[64:], 96, 1)
 
@@ -529,23 +540,29 @@
 
     lax.fori_loop(1, NT, sent_b, 0)
 
-
-def finish(first, pixels, facts, over_t, lone_t, over_j):
+    def sent_a(i, _):
+        give_rows(lax.rem(me + i, NT)).wait_send()
+        return 0
+
+    lax.fori_loop(1, NT, sent_a, 0)
+
+
+def finish(first, half, facts, over_x, over_t, lone_t, over_j):
     vmem = pl.BlockSpec(memory_space=pltpu.VMEM)
     shapes, outs = [jax.ShapeDtypeStruct((64, 128), F32)], [vmem]
     scratch = [
+        pltpu.VMEM((4096, 128), F32),
+        pltpu.VMEM((NT * ROWS, 128), BF),
         pltpu.VMEM((NT * ROWS, 128), BF),
         pltpu.VMEM((NT * WS, 128), F32),
         pltpu.VMEM((32 * MS, 128), F32),
         pltpu.VMEM((NT, 128), F32),
         pltpu.VMEM((256, 128), F32),
         pltpu.VMEM((256, 128), F32),
-        pltpu.VMEM((2048, 256), BF),
         pltpu.SemaphoreType.DMA((NT,)),
         pltpu.SemaphoreType.DMA((NT,)),
         pltpu.SemaphoreType.DMA((NT,)),
         pltpu.SemaphoreType.DMA((NT,)),
-        pltpu.SemaphoreType.DMA,
     ]
     if first:
         shapes.append(jax.ShapeDtypeStruct((1, 1), F32))
@@ -559,14 +576,14 @@
     return pl.pallas_call(
         functools.partial(finish_body, first),
         out_shape=shapes,
-        in_specs=[vmem] * 4 + [pl.BlockSpec(memory_space=pltpu.HBM)],
+        in_specs=[vmem] * 6,
         out_specs=outs,
         scratch_shapes=scratch,
         compiler_params=pltpu.CompilerParams(
-            collective_id=1 if first else 3, has_side_effects=True, vmem_limit_bytes=60 * MIB
+            collective_id=1 if first else 3, has_side_effects=True, vmem_limit_bytes=20 * MIB
         ),
         name="finish" if first else "finish_more",
-    )(pixels, facts, over_t, lone_t, over_j)
+    )(half, facts, over_x, over_t, lone_t, over_j)
 
 
 def local(visibilities, kernels, destination, cell, plane):
@@ -575,10 +592,9 @@
     samples = visibilities[0]
     dest = destination.reshape(1, BLK)
     kern = kernels.reshape(NW * 128, 128)
-    none = jnp.zeros((1, BLK), jnp.int32)
-    recv, facts, table, weight = exchange(True, samples, dest, cell, plane, none, kern)
-    pixels = grid_and_rows(facts, recv, table, weight, over_r, over_x)
-    image, most = finish(True, pixels, facts, over_t, lone_t, over_j)
+    recv, facts, table, weight = exchange(True, samples, dest, cell, plane, kern)
+    half = grid_and_rows(facts, recv, table, weight, over_r)
+    image, most = finish(True, half, facts, over_x, over_t, lone_t, over_j)
     most = most[0, 0]
 
     def more(image):
@@ -586,8 +602,8 @@
             done, total = state
             skipped = jnp.broadcast_to(done, (1, BLK))
             recv, facts = exchange(False, samples, dest, cell, plane, skipped)
-            pixels = grid_and_rows(facts, recv, table, weight, over_r, over_x)
-            [terms] = finish(False, pixels, facts, over_t, lone_t, over_j)
+            half = grid_and_rows(facts, recv, table, weight, over_r)
+            [terms] = finish(False, half, facts, over_x, over_t, lone_t, over_j)
             return done + CAP, total + terms
 
         return lax.while_loop(

time: 66.2 us -> 58.4 us (0.88)
  Pallas kernels: 63.8 us -> 55.2 us
    pallas_call x1, Pallas kernels: 18.7 us -> 12.3 us  [grid_and_rows(): pl.pallas_call(grid_body, out_shape=HALF, in_specs=[pl.BlockSpec(memory_s...]
    pallas_call x1, Pallas kernels: 29 us -> 27.6 us  [finish(): pl.pallas_call(functools.partial(finish_body, first), out_shape=shapes, i...]
    unnamed x16 -> x22, local copies, waits for them, and re-layouts: 0.05 us -> 1.28 us
    pallas_call x1, Pallas kernels: 16.1 us -> 15.3 us  [exchange(): pl.pallas_call(functools.partial(exchange_body, first), out_shape=shapes,...]
where the time goes in v4:
time: 58.4 us; the launch traced here: 58.2 us
  Pallas kernels  55.2 us (95%)
  local copies, waits for them, and re-layouts  2.18 us (4%)
  between operations  0.86 us (1%)
    pallas_call x1, Pallas kernels, finish(): pl.pallas_call(functools.partial(finish_body, first), out_shape=shapes, i...  27.6 us
    pallas_call x1, Pallas kernels, exchange(): pl.pallas_call(functools.partial(exchange_body, first), out_shape=shapes,...  15.3 us
    pallas_call x1, Pallas kernels, grid_and_rows(): pl.pallas_call(grid_body, out_shape=HALF, in_specs=[pl.BlockSpec(memory_s...  12.3 us
    unnamed x22, local copies, waits for them, and re-layouts  1.28 us

profile of v4, /device:TPU:1, one launch (start us, length us, event | category | flops | bytes accessed | tf_op | source)
XLA Modules:
  0.0 58.2 jit_solution(10858030950186252221)
XLA Ops:
  0.0 0.0 copy-start
  0.0 1.2 %copy-done = bf16[1,32,2,64,128]{4,3,2,1,0:T(8,128)(2,1)S(1)} copy-done((bf16[1,32,2,64,128]{4,3,2,1,0:T(8,128)(2,1)S(1)}, bf16[1,32,2,64,128]{4,3,2,1,0:T(8,128)(2,1)}, u32[]{:S(2)}) %copy-start) | copy-done | bytes 1048600
  1.2 0.0 copy-start.2
  1.2 0.0 copy-start.3
  1.2 0.0 copy-start.7
  1.2 0.0 copy-start.8
  1.2 15.3 %exchange.1 = (bf16[1024,128]{1,0:T(8,128)(2,1)S(1)}, s32[32,128]{1,0:T(8,128)S(1)}, f32[4096,128]{1,0:T(8,128)S(1)}, bf16[8192,128]{1,0:T(8,128)(2,1)S(1)}) custom-call(f32[256,128]{1,0:T(8,128)} %bitcast.12, s32[1,256]{1,0:T(1,128)} %bitcast.15, s32[1,256]{1,0:T(1,128)} %cell.1, s32[1,256]{1,0:T(1,128)} %plane.1, bf16[4096,128]{1,0:T(8,128)(2,1)S(1)} %bitcast.11), custom_call_target="tpu_custom_call" | custom-call | tf_op jit(solution)/shard_map/exchange/pallas_call | solution.py:209
  16.5 0.0 copy-start.1
  16.5 0.0 copy-start.5
  16.5 0.0 copy-start.6
  16.5 0.0 copy-start.9
  16.5 0.0 copy-start.10
  16.6 0.0 copy-start.11
  16.6 12.3 %grid_and_rows.2.half = f32[33024,128]{1,0:T(8,128)S(1)} custom-call(s32[32,128]{1,0:T(8,128)S(1)} %get-tuple-element.129.facts, bf16[1024,128]{1,0:T(8,128)(2,1)S(1)} %get-tuple-element.130.recv, f32[4096,128]{1,0:T(8,128)S(1)} %get-tuple-element.131.table, bf16[8192,128]{1,0:T(8,128)(2,1)S(1)} %get-tuple-element.132.weight, ...), custom_call_target="tpu_custom_call" | custom-call | tf_op jit(solution)/shard_map/grid_and_rows/pallas_call | solution.py:278
  28.8 0.0 copy-done.2
  28.9 0.0 copy-done.3
  28.9 0.0 copy-done.7
  28.9 0.0 copy-done.8
  28.9 27.6 %finish.1 = (f32[64,128]{1,0:T(8,128)S(1)}, f32[1,1]{1,0:T(1,128)}) custom-call(f32[33024,128]{1,0:T(8,128)S(1)} %grid_and_rows.2.half, s32[32,128]{1,0:T(8,128)S(1)} %get-tuple-element.129.facts, bf16[4096,128]{1,0:T(8,128)(2,1)S(1)} %copy-done.3, bf16[256,64]{1,0:T(8,128)(2,1)S(1)} %copy-done.7, bf16[128,32]{1,0:T(8,128)(2,1)S(1)} %copy-done.8, ...), custom_call_target="tpu_custom_call" | custom-call | tf_op jit(solution)/shard_map/finish/pallas_call | solution.py:576
  56.5 0.0 copy-done.1
  57.2 0.0 copy-done.5
  57.2 0.0 copy-done.6
  57.2 0.0 copy-done.9
  57.3 0.0 copy-done.10
  57.3 0.0 copy-done.11
  57.3 0.1 reshape.14
  57.4 0.1 copy.13
  57.5 0.7 %reshape.15 = f32[256,32]{0,1:T(8,128)} reshape(f32[8,32,4,8]{1,0,3,2:T(8,128)S(1)} %bitcast.14) | data formatting | bytes 65536 | tf_op jit(solution)/shard_map/reshape | solution.py:614
  (1 shorter events, 0.0 us)
Async XLA Ops:
  0.0 1.2 %copy-start = (bf16[1,32,2,64,128]{4,3,2,1,0:T(8,128)(2,1)S(1)}, bf16[1,32,2,64,128]{4,3,2,1,0:T(8,128)(2,1)}, u32[]{:S(2)}) copy-start(bf16[1,32,2,64,128]{4,3,2,1,0:T(8,128)(2,1)} %param.15) | copy-start | bytes 3145732
  1.2 27.6 %copy-start.2 = (bf16[2048,256]{1,0:T(8,128)(2,1)S(1)}, bf16[2048,256]{1,0:T(8,128)(2,1)}, u32[]{:S(2)}) copy-start(bf16[2048,256]{1,0:T(8,128)(2,1)} %constant.19.clone.over_j) | copy-start | bytes 3145732
  1.2 27.6 %copy-start.3 = (bf16[4096,128]{1,0:T(8,128)(2,1)S(1)}, bf16[4096,128]{1,0:T(8,128)(2,1)}, u32[]{:S(2)}) copy-start(bf16[4096,128]{1,0:T(8,128)(2,1)} %constant.17.clone.over_x) | copy-start | bytes 3145732
  1.2 27.6 %copy-start.7 = (bf16[256,64]{1,0:T(8,128)(2,1)S(1)}, bf16[256,64]{1,0:T(8,128)(2,1)}, u32[]{:S(2)}) copy-start(bf16[256,64]{1,0:T(8,128)(2,1)} %constant.18.clone.over_t) | copy-start | bytes 98308
  1.2 27.6 %copy-start.8 = (bf16[128,32]{1,0:T(8,128)(2,1)S(1)}, bf16[128,32]{1,0:T(8,128)(2,1)}, u32[]{:S(2)}) copy-start(bf16[128,32]{1,0:T(8,128)(2,1)} %constant.20.clone.lone_t) | copy-start | bytes 24580
  16.5 40.0 %copy-start.1 = (bf16[8192,128]{1,0:T(8,128)(2,1)}, bf16[8192,128]{1,0:T(8,128)(2,1)S(1)}, u32[]{:S(2)}) copy-start(bf16[8192,128]{1,0:T(8,128)(2,1)S(1)} %get-tuple-element.132.weight) | copy-start | bytes 6291460
  16.5 40.7 %copy-start.5 = (bf16[256,256]{1,0:T(8,128)(2,1)S(1)}, bf16[256,256]{1,0:T(8,128)(2,1)}, u32[]{:S(2)}) copy-start(bf16[256,256]{1,0:T(8,128)(2,1)} %constant.16.clone.over_r) | copy-start | bytes 393220
  16.5 40.7 %copy-start.6 = (f32[1,256,128]{2,1,0:T(8,128)S(1)}, f32[1,256,128]{2,1,0:T(8,128)}, u32[]{:S(2)}) copy-start(f32[1,256,128]{2,1,0:T(8,128)} %param.14) | copy-start | bytes 393220
  16.5 40.7 %copy-start.9 = (s32[1,256,1]{1,2,0:T(1,128)S(1)}, s32[1,256,1]{1,2,0:T(1,128)}, u32[]{:S(2)}) copy-start(s32[1,256,1]{1,2,0:T(1,128)} %param.16) | copy-start | bytes 3076
  16.5 40.7 %copy-start.10 = (s32[1,256]{1,0:T(1,128)S(1)}, s32[1,256]{1,0:T(1,128)}, u32[]{:S(2)}) copy-start(s32[1,256]{1,0:T(1,128)} %cell.1) | copy-start | bytes 3076
  16.6 40.7 %copy-start.11 = (s32[1,256]{1,0:T(1,128)S(1)}, s32[1,256]{1,0:T(1,128)}, u32[]{:S(2)}) copy-start(s32[1,256]{1,0:T(1,128)} %plane.1) | copy-start | bytes 3076

commit v5 on v4

--- a/solution.py
+++ b/solution.py
@@ -20,17 +20,15 @@
 CAP = 31
 GS = 65
 HS = 129
-TOGETHER = 32
+TOGETHER = 48
 WS = 65
 MS = 129
-ROWS = 80
 SLOTS = 32
 ALL = NT * SLOTS
 MIB = 1 << 20
 BF = jnp.bfloat16
 F32 = jnp.float32
 MESH = pl.DeviceIdType.MESH
-HALF = jax.ShapeDtypeStruct((2 * 128 * HS, 128), F32)
 
 
 def split(table):
@@ -219,7 +217,7 @@
     )(*operands)
 
 
-def grid_body(facts, recv, table, weight, over_r, half, grid, fill_a, fill_b, todo):
+def grid_body(facts, recv, table, weight, grid, fill_a, fill_b, todo):
     lane = iota((ALL, 128), 1)
     slot = iota((ALL, 128), 0)
     blocks = jnp.where(jnp.bitwise_and(slot, SLOTS - 1) == CAP, 0.0, recv[...].astype(F32))
@@ -259,6 +257,63 @@
 
     lax.fori_loop(0, (number + TOGETHER - 1) // TOGETHER, blocks_together, 0)
 
+
+def add_blocks(facts, recv, table, weight):
+    vmem = pl.BlockSpec(memory_space=pltpu.VMEM)
+    return pl.pallas_call(
+        grid_body,
+        out_shape=jax.ShapeDtypeStruct((512 * GS, 128), F32),
+        in_specs=[pl.BlockSpec(memory_space=pltpu.SMEM)] + [vmem] * 3,
+        out_specs=vmem,
+        scratch_shapes=[
+            pltpu.VMEM((ALL, 128), F32),
+            pltpu.VMEM((ALL, 128), F32),
+            pltpu.SMEM((ALL + 64,), jnp.int32),
+        ],
+        compiler_params=pltpu.CompilerParams(vmem_limit_bytes=8 * MIB),
+        name="add_blocks",
+    )(facts, recv, table, weight)
+
+
+def finish_body(first, grid, facts, over_r, over_x, over_t, lone_t, over_j, *rest):
+    if first:
+        out, most, *rest, mine, seen, send_y, recv_y = rest
+    else:
+        out, *rest = rest
+    half, pixels, send, recv, wide, middle, alone, lone, fold, last, *sems = rest
+    send_a, recv_a, send_b, recv_b, send_c, recv_c = sems
+    me = lax.axis_index("tile")
+    chan = lax.axis_index("chan")
+    home = me // 8
+    stays = home == chan
+    barrier = pltpu.get_barrier_semaphore()
+
+    def greet(i, _):
+        pl.semaphore_signal(
+            barrier, inc=1, device_id=(lax.rem(me + i, NT), chan), device_id_type=MESH
+        )
+        return 0
+
+    lax.fori_loop(1, NT, greet, 0)
+
+    def greet_source(i, _):
+        from_t, from_c = chan * 8 + i // NC, lax.rem(i, NC)
+
+        @pl.when(jnp.logical_or(from_t != me, from_c != chan))
+        def _():
+            pl.semaphore_signal(barrier, inc=1, device_id=(from_t, from_c), device_id_type=MESH)
+
+        return 0
+
+    lax.fori_loop(0, NT, greet_source, 0)
+    greeted = 2 * NT - 1
+    if first:
+        greeted += NC - 1
+        for i in range(1, NC):
+            pl.semaphore_signal(
+                barrier, inc=1, device_id=(me, lax.rem(chan + i, NC)), device_id_type=MESH
+            )
+
     def over_rows(x, _):
         part = [grid[pl.ds(i * 128 * GS + x, 128, stride=GS), :] for i in range(4)]
         real = jnp.concatenate([p[:, :S] for p in part], axis=1)
@@ -270,69 +325,12 @@
         half[pl.ds(128 * HS + S + x, 128, stride=HS), :] = got[128:, 128:]
         return 0
 
-    lax.fori_loop(0, S, over_rows, 0, unroll=8)
-
-
-def grid_and_rows(facts, recv, table, weight, over_r):
-    vmem = pl.BlockSpec(memory_space=pltpu.VMEM)
-    return pl.pallas_call(
-        grid_body,
-        out_shape=HALF,
-        in_specs=[pl.BlockSpec(memory_space=pltpu.SMEM)] + [vmem] * 4,
-        out_specs=vmem,
-        scratch_shapes=[
-            pltpu.VMEM((512 * GS, 128), F32),
-            pltpu.VMEM((ALL, 128), F32),
-            pltpu.VMEM((ALL, 128), F32),
-            pltpu.SMEM((ALL + 64,), jnp.int32),
-        ],
-        compiler_params=pltpu.CompilerParams(vmem_limit_bytes=24 * MIB),
-        name="grid_and_rows",
-    )(facts, recv, table, weight, over_r)
-
-
-def finish_body(first, half, facts, over_x, over_t, lone_t, over_j, *rest):
-    if first:
-        out, most, *rest, mine, seen, send_y, recv_y = rest
-    else:
-        out, *rest = rest
-    pixels, send, recv, wide, middle, lone, fold, last, send_a, recv_a, send_b, recv_b = rest
-    me = lax.axis_index("tile")
-    chan = lax.axis_index("chan")
-    home = me // 8
-    stays = home == chan
-    barrier = pltpu.get_barrier_semaphore()
-
-    def greet(i, _):
-        pl.semaphore_signal(
-            barrier, inc=1, device_id=(lax.rem(me + i, NT), chan), device_id_type=MESH
-        )
-        return 0
-
-    lax.fori_loop(1, NT, greet, 0)
-
-    def greet_source(i, _):
-        from_t, from_c = chan * 8 + i // NC, lax.rem(i, NC)
-
-        @pl.when(jnp.logical_or(from_t != me, from_c != chan))
-        def _():
-            pl.semaphore_signal(barrier, inc=1, device_id=(from_t, from_c), device_id_type=MESH)
-
-        return 0
-
-    lax.fori_loop(0, NT, greet_source, 0)
-    greeted = 2 * NT - 1
-    if first:
-        greeted += NC - 1
-        for i in range(1, NC):
-            pl.semaphore_signal(
-                barrier, inc=1, device_id=(me, lax.rem(chan + i, NC)), device_id_type=MESH
-            )
+    lax.fori_loop(0, S, over_rows, 0, unroll=32)
 
     def give_rows(to):
         return pltpu.make_async_remote_copy(
-            src_ref=send.at[pl.ds(pl.multiple_of(to * ROWS, 16), ROWS)],
-            dst_ref=recv.at[pl.ds(pl.multiple_of(me * ROWS, 16), ROWS)],
+            src_ref=send.at[pl.ds(pl.multiple_of(to * 64, 64), 64)],
+            dst_ref=recv.at[pl.ds(pl.multiple_of(me * 64, 64), 64)],
             send_sem=send_a.at[to],
             recv_sem=recv_a.at[me],
             device_id=(to, chan),
@@ -340,12 +338,32 @@
         )
 
     def take_rows(source):
-        at = pl.ds(pl.multiple_of(source * ROWS, 16), ROWS)
+        at = pl.ds(pl.multiple_of(source * 64, 64), 64)
         return pltpu.make_async_remote_copy(
             src_ref=recv.at[at],
             dst_ref=recv.at[at],
             send_sem=send_a.at[source],
             recv_sem=recv_a.at[source],
+            device_id=(source, chan),
+            device_id_type=MESH,
+        )
+
+    def give_alone(to):
+        return pltpu.make_async_remote_copy(
+            src_ref=alone.at[to],
+            dst_ref=lone.at[me],
+            send_sem=send_c.at[to],
+            recv_sem=recv_c.at[me],
+            device_id=(to, chan),
+            device_id_type=MESH,
+        )
+
+    def take_alone(source):
+        return pltpu.make_async_remote_copy(
+            src_ref=lone.at[source],
+            dst_ref=lone.at[source],
+            send_sem=send_c.at[source],
+            recv_sem=recv_c.at[source],
             device_id=(source, chan),
             device_id_type=MESH,
         )
@@ -373,8 +391,7 @@
         to = jnp.bitwise_and(i + me // 4, 7) * 4 + part
         rows = pl.multiple_of(to * 64, 64)
         mirror = pixels[pl.ds(2048 + rows, 64), :]
-        at = pl.multiple_of(to * ROWS, 16)
-        send[pl.ds(at, 64), :] = (
+        send[pl.ds(rows, 64), :] = (
             pixels[pl.ds(rows, 64), :] + jnp.where(past, mirror, 0.0)
         ).astype(BF)
         spread = jnp.zeros((32, 128), F32)
@@ -383,8 +400,7 @@
             spread = jnp.where(
                 lane == place + 32 * q, jnp.broadcast_to(column, (32, 128)), spread
             )
-        spread = jnp.sum(spread, axis=0, keepdims=True)
-        send[pl.ds(at + 64, 16), :] = jnp.broadcast_to(spread, (16, 128)).astype(BF)
+        alone[to] = jnp.sum(spread, axis=0, keepdims=True)
         return part
 
     def start(i, part):
@@ -393,6 +409,7 @@
         @pl.when(to != me)
         def _():
             give_rows(to).start()
+            give_alone(to).start()
 
         return part
 
@@ -405,7 +422,7 @@
             return part
 
         lax.fori_loop(0, 2, some, part)
-        lax.fori_loop(0, 8, pack, part, unroll=2)
+        lax.fori_loop(0, 8, pack, part, unroll=8)
         if turn == 0:
             pl.semaphore_wait(barrier, jnp.where(stays, greeted - 1, greeted))
         lax.fori_loop(0, 8, start, part)
@@ -426,19 +443,20 @@
 
         for i in range(1, NC):
             tell(i).start()
-    own = pl.ds(pl.multiple_of(me * ROWS, 16), ROWS)
+    own = pl.ds(pl.multiple_of(me * 64, 64), 64)
     recv[own, :] = send[own, :]
+    lone[me] = alone[me]
 
     def wait(i, _):
         take_rows(lax.rem(me + i, NT)).wait_recv()
+        take_alone(lax.rem(me + i, NT)).wait_recv()
         return 0
 
     lax.fori_loop(1, NT, wait, 0)
 
     def widen(t, _):
-        block = recv[pl.ds(pl.multiple_of(t * ROWS, 16), ROWS), :].astype(F32)
-        wide[pl.ds(t * WS, 64), :] = block[:64]
-        lone[pl.ds(t, 1), :] = block[64:65]
+        block = recv[pl.ds(pl.multiple_of(t * 64, 64), 64), :].astype(F32)
+        wide[pl.ds(t * WS, 64), :] = block
         return 0
 
     lax.fori_loop(0, NT, widen, 0, unroll=4)
@@ -450,35 +468,32 @@
         return 0
 
     lax.fori_loop(0, 32, over_tiles, 0, unroll=8)
-    alone = dot(lone_t[...], lone[...].astype(BF))
-    wide[0:64, :] = alone[:64] - pltpu.roll(alone[64:], 96, 1)
-
-    def over_columns(a, _):
-        for h in range(2):
-            made = []
-            for b in range(4):
-                m0 = h * 32 + b * 8 + a
-                right = jnp.concatenate(
-                    [middle[pl.ds(64 * q + m0, 32, stride=MS), :] for q in range(2)], axis=1
-                )
-                high = right.astype(BF)
-                low = (right - high.astype(F32)).astype(BF)
-                left = over_j[pl.ds(pl.multiple_of(m0 * 32, 32), 32), :]
-                got = dot_t(left, high)
-                got = got[:16] + got[16:] + dot_t(left[:16], low)
-                made.append(got + wide[pl.ds(m0, 1), :][:, :32])
-            fold[pl.ds(h * 8 + a, 16, stride=16), :] = jnp.concatenate(made, axis=1)
-        return 0
-
-    lax.fori_loop(0, 8, over_columns, 0, unroll=2)
+    added = dot(lone_t[...], lone[...].reshape(NT, 128).astype(BF))
+    wide[0:64, :] = added[:64] - pltpu.roll(added[64:], 96, 1)
+
+    def over_columns(a, h):
+        made = []
+        for b in range(4):
+            m0 = h * 32 + b * 8 + a
+            right = jnp.concatenate(
+                [middle[pl.ds(64 * q + m0, 32, stride=MS), :] for q in range(2)], axis=1
+            )
+            high = right.astype(BF)
+            low = (right - high.astype(F32)).astype(BF)
+            left = over_j[pl.ds(pl.multiple_of(m0 * 32, 32), 32), :]
+            got = dot_t(left, high)
+            got = got[:16] + got[16:] + dot_t(left[:16], low)
+            made.append(got + wide[pl.ds(m0, 1), :][:, :32])
+        fold[pl.ds(h * 8 + a, 16, stride=16), :] = jnp.concatenate(made, axis=1)
+        return h
+
     slot = lax.rem(me, 8) * NC + chan
 
-    def give(i):
-        to = lax.rem(me + i, NT)
+    def give(to):
         return pltpu.make_async_remote_copy(
             src_ref=fold.at[pl.ds(pl.multiple_of(to * 8, 8), 8)],
             dst_ref=last.at[pl.ds(pl.multiple_of(slot * 8, 8), 8)],
-            send_sem=send_b.at[i],
+            send_sem=send_b.at[to],
             recv_sem=recv_b.at[slot],
             device_id=(to, home),
             device_id_type=MESH,
@@ -495,9 +510,18 @@
             device_id_type=MESH,
         )
 
-    @pl.when(jnp.logical_not(stays))
-    def _():
-        give(0).start()
+    def start_b(i, h):
+        to = 2 * jnp.bitwise_and(i + me // 2, 15) + h
+
+        @pl.when(jnp.logical_or(jnp.logical_not(stays), to != me))
+        def _():
+            give(to).start()
+
+        return h
+
+    for h in range(2):
+        lax.fori_loop(0, 8, over_columns, h, unroll=4)
+        lax.fori_loop(0, 16, start_b, h)
 
     @pl.when(stays)
     def _():
@@ -505,11 +529,6 @@
             pl.ds(pl.multiple_of(me * 8, 8), 8), :
         ]
 
-    def start_b(i, _):
-        give(i).start()
-        return 0
-
-    lax.fori_loop(1, NT, start_b, 0)
     if first:
         for i in range(1, NC):
             tell(i).wait()
@@ -524,41 +543,50 @@
         return 0
 
     lax.fori_loop(0, NT, wait_b, 0)
+    totals = []
     for t in range(8):
         total = last[t * 32 : t * 32 + 8, :]
         for c in range(1, NC):
             total = total + last[t * 32 + c * 8 : t * 32 + c * 8 + 8, :]
-        out[t * 8 : t * 8 + 8, :] = total
-
-    @pl.when(jnp.logical_not(stays))
-    def _():
-        give(0).wait_send()
+        totals.append(total)
+    for b in range(4):
+        out[b * 8 : b * 8 + 8, :] = jnp.concatenate(
+            [total[:, b * 32 : b * 32 + 32] for total in totals], axis=1
+        )
 
     def sent_b(i, _):
-        give(i).wait_send()
-        return 0
-
-    lax.fori_loop(1, NT, sent_b, 0)
+        @pl.when(jnp.logical_or(jnp.logical_not(stays), i != me))
+        def _():
+            give(i).wait_send()
+
+        return 0
+
+    lax.fori_loop(0, NT, sent_b, 0)
 
     def sent_a(i, _):
         give_rows(lax.rem(me + i, NT)).wait_send()
+        give_alone(lax.rem(me + i, NT)).wait_send()
         return 0
 
     lax.fori_loop(1, NT, sent_a, 0)
 
 
-def finish(first, half, facts, over_x, over_t, lone_t, over_j):
+def finish(first, grid, facts, over_r, over_x, over_t, lone_t, over_j):
     vmem = pl.BlockSpec(memory_space=pltpu.VMEM)
-    shapes, outs = [jax.ShapeDtypeStruct((64, 128), F32)], [vmem]
+    shapes, outs = [jax.ShapeDtypeStruct((32, 256), F32)], [vmem]
     scratch = [
+        pltpu.VMEM((2 * 128 * HS, 128), F32),
         pltpu.VMEM((4096, 128), F32),
-        pltpu.VMEM((NT * ROWS, 128), BF),
-        pltpu.VMEM((NT * ROWS, 128), BF),
+        pltpu.VMEM((NT * 64, 128), BF),
+        pltpu.VMEM((NT * 64, 128), BF),
         pltpu.VMEM((NT * WS, 128), F32),
         pltpu.VMEM((32 * MS, 128), F32),
-        pltpu.VMEM((NT, 128), F32),
+        pltpu.VMEM((NT, 1, 128), F32),
+        pltpu.VMEM((NT, 1, 128), F32),
         pltpu.VMEM((256, 128), F32),
         pltpu.VMEM((256, 128), F32),
+        pltpu.SemaphoreType.DMA((NT,)),
+        pltpu.SemaphoreType.DMA((NT,)),
         pltpu.SemaphoreType.DMA((NT,)),
         pltpu.SemaphoreType.DMA((NT,)),
         pltpu.SemaphoreType.DMA((NT,)),
@@ -576,14 +604,14 @@
     return pl.pallas_call(
         functools.partial(finish_body, first),
         out_shape=shapes,
-        in_specs=[vmem] * 6,
+        in_specs=[vmem] * 7,
         out_specs=outs,
         scratch_shapes=scratch,
         compiler_params=pltpu.CompilerParams(
-            collective_id=1 if first else 3, has_side_effects=True, vmem_limit_bytes=20 * MIB
+            collective_id=1 if first else 3, has_side_effects=True, vmem_limit_bytes=30 * MIB
         ),
         name="finish" if first else "finish_more",
-    )(half, facts, over_x, over_t, lone_t, over_j)
+    )(grid, facts, over_r, over_x, over_t, lone_t, over_j)
 
 
 def local(visibilities, kernels, destination, cell, plane):
@@ -593,8 +621,8 @@
     dest = destination.reshape(1, BLK)
     kern = kernels.reshape(NW * 128, 128)
     recv, facts, table, weight = exchange(True, samples, dest, cell, plane, kern)
-    half = grid_and_rows(facts, recv, table, weight, over_r)
-    image, most = finish(True, half, facts, over_x, over_t, lone_t, over_j)
+    grid = add_blocks(facts, recv, table, weight)
+    image, most = finish(True, grid, facts, over_r, over_x, over_t, lone_t, over_j)
     most = most[0, 0]
 
     def more(image):
@@ -602,8 +630,8 @@
             done, total = state
             skipped = jnp.broadcast_to(done, (1, BLK))
             recv, facts = exchange(False, samples, dest, cell, plane, skipped)
-            half = grid_and_rows(facts, recv, table, weight, over_r)
-            [terms] = finish(False, half, facts, over_x, over_t, lone_t, over_j)
+            grid = add_blocks(facts, recv, table, weight)
+            [terms] = finish(False, grid, facts, over_r, over_x, over_t, lone_t, over_j)
             return done + CAP, total + terms
 
         return lax.while_loop(
@@ -611,7 +639,7 @@
         )[1]
 
     image = lax.cond(most > CAP, more, lambda terms: terms, image)
-    return image.reshape(8, 8, 4, 32).transpose(0, 3, 2, 1).reshape(256, 32)
+    return image.T
 
 
 def solution(mesh):

time: 58.4 us -> 53.7 us (0.920)
  Pallas kernels: 55.2 us -> 50.6 us
    pallas_call x1, Pallas kernels: 12.3 us -> 7.08 us  [add_blocks(): pl.pallas_call(grid_body, out_shape=jax.ShapeDtypeStruct((512 * GS, 128),...]
    reshape x3 -> x0, local copies, waits for them, and re-layouts: 0.91 us -> none  [local(): return image.reshape(8, 8, 4, 32).transpose(0, 3, 2, 1).reshape(256, 32)]
    pallas_call x1, Pallas kernels: 27.6 us -> 28.3 us  [finish(): pl.pallas_call(functools.partial(finish_body, first), out_shape=shapes, i...]
    unnamed x22 -> x23, local copies, waits for them, and re-layouts: 1.28 us -> 1.89 us
where the time goes in v5:
time: 53.7 us; the launch traced here: 53.6 us
  Pallas kernels  50.6 us (94%)
  local copies, waits for them, and re-layouts  1.89 us (4%)
  between operations  0.85 us (2%)
    pallas_call x1, Pallas kernels, finish(): pl.pallas_call(functools.partial(finish_body, first), out_shape=shapes, i...  28.3 us
    pallas_call x1, Pallas kernels, exchange(): pl.pallas_call(functools.partial(exchange_body, first), out_shape=shapes,...  15.3 us
    pallas_call x1, Pallas kernels, add_blocks(): pl.pallas_call(grid_body, out_shape=jax.ShapeDtypeStruct((512 * GS, 128),...  7.08 us
    unnamed x23, local copies, waits for them, and re-layouts  1.89 us

profile of v5, /device:TPU:1, one launch (start us, length us, event | category | flops | bytes accessed | tf_op | source)
XLA Modules:
  0.0 53.6 jit_solution(872229233603546683)
XLA Ops:
  0.0 0.0 copy-start
  0.0 1.2 %copy-done = bf16[1,32,2,64,128]{4,3,2,1,0:T(8,128)(2,1)S(1)} copy-done((bf16[1,32,2,64,128]{4,3,2,1,0:T(8,128)(2,1)S(1)}, bf16[1,32,2,64,128]{4,3,2,1,0:T(8,128)(2,1)}, u32[]{:S(2)}) %copy-start) | copy-done | bytes 1048600
  1.2 0.0 copy-start.2
  1.2 0.0 copy-start.3
  1.2 0.0 copy-start.5
  1.2 0.0 copy-start.7
  1.2 0.0 copy-start.8
  1.2 15.3 %exchange.1 = (bf16[1024,128]{1,0:T(8,128)(2,1)S(1)}, s32[32,128]{1,0:T(8,128)S(1)}, f32[4096,128]{1,0:T(8,128)S(1)}, bf16[8192,128]{1,0:T(8,128)(2,1)S(1)}) custom-call(f32[256,128]{1,0:T(8,128)} %bitcast.6, s32[1,256]{1,0:T(1,128)} %bitcast.9, s32[1,256]{1,0:T(1,128)} %cell.1, s32[1,256]{1,0:T(1,128)} %plane.1, bf16[4096,128]{1,0:T(8,128)(2,1)S(1)} %bitcast.5), custom_call_target="tpu_custom_call" | custom-call | tf_op jit(solution)/shard_map/exchange/pallas_call | solution.py:207
  16.5 0.0 copy-start.1
  16.5 0.0 copy-start.6
  16.5 0.0 copy-start.9
  16.5 0.0 copy-start.10
  16.6 0.0 copy-start.11
  16.6 7.1 %add_blocks.2.grid = f32[33280,128]{1,0:T(8,128)S(1)} custom-call(s32[32,128]{1,0:T(8,128)S(1)} %get-tuple-element.129.facts, bf16[1024,128]{1,0:T(8,128)(2,1)S(1)} %get-tuple-element.130.recv, f32[4096,128]{1,0:T(8,128)S(1)} %get-tuple-element.131.table, bf16[8192,128]{1,0:T(8,128)(2,1)S(1)} %get-tuple-element.132.weight), custom_call_target="tpu_custom_call" | custom-call | tf_op jit(solution)/shard_map/add_blocks/pallas_call | solution.py:263
  23.7 0.0 copy-done.2
  23.7 0.0 copy-done.3
  23.7 0.0 copy-done.5
  23.7 0.0 copy-done.7
  23.7 0.0 copy-done.8
  23.7 28.3 %finish.1 = (f32[32,256]{1,0:T(8,128)S(1)}, f32[1,1]{1,0:T(1,128)}) custom-call(f32[33280,128]{1,0:T(8,128)S(1)} %add_blocks.2.grid, s32[32,128]{1,0:T(8,128)S(1)} %get-tuple-element.129.facts, bf16[256,256]{1,0:T(8,128)(2,1)S(1)} %copy-done.5, bf16[4096,128]{1,0:T(8,128)(2,1)S(1)} %copy-done.3, bf16[256,64]{1,0:T(8,128)(2,1)S(1)} %copy-done.7, ...), custom_call_target="tpu_custom_call" | custom-call | tf_op jit(solution)/shard_map/finish/pallas_call | solution.py:604
  52.0 0.0 copy-done.1
  52.7 0.0 copy-done.6
  52.7 0.0 copy-done.9
  52.7 0.0 copy-done.10
  52.7 0.0 copy-done.11
  52.7 0.2 conditional.1
  52.9 0.6 %copy.20 = f32[256,32]{0,1:T(8,128)} copy(f32[256,32]{0,1:T(8,128)S(1)} %bitcast.8) | data formatting | bytes 65536
Async XLA Ops:
  0.0 1.2 %copy-start = (bf16[1,32,2,64,128]{4,3,2,1,0:T(8,128)(2,1)S(1)}, bf16[1,32,2,64,128]{4,3,2,1,0:T(8,128)(2,1)}, u32[]{:S(2)}) copy-start(bf16[1,32,2,64,128]{4,3,2,1,0:T(8,128)(2,1)} %param.15) | copy-start | bytes 3145732
  1.2 22.4 %copy-start.2 = (bf16[2048,256]{1,0:T(8,128)(2,1)S(1)}, bf16[2048,256]{1,0:T(8,128)(2,1)}, u32[]{:S(2)}) copy-start(bf16[2048,256]{1,0:T(8,128)(2,1)} %constant.19.clone.over_j) | copy-start | bytes 3145732
  1.2 22.4 %copy-start.3 = (bf16[4096,128]{1,0:T(8,128)(2,1)S(1)}, bf16[4096,128]{1,0:T(8,128)(2,1)}, u32[]{:S(2)}) copy-start(bf16[4096,128]{1,0:T(8,128)(2,1)} %constant.17.clone.over_x) | copy-start | bytes 3145732
  1.2 22.4 %copy-start.5 = (bf16[256,256]{1,0:T(8,128)(2,1)S(1)}, bf16[256,256]{1,0:T(8,128)(2,1)}, u32[]{:S(2)}) copy-start(bf16[256,256]{1,0:T(8,128)(2,1)} %constant.16.clone.over_r) | copy-start | bytes 393220
  1.2 22.5 %copy-start.7 = (bf16[256,64]{1,0:T(8,128)(2,1)S(1)}, bf16[256,64]{1,0:T(8,128)(2,1)}, u32[]{:S(2)}) copy-start(bf16[256,64]{1,0:T(8,128)(2,1)} %constant.18.clone.over_t) | copy-start | bytes 98308
  1.2 22.5 %copy-start.8 = (bf16[128,32]{1,0:T(8,128)(2,1)S(1)}, bf16[128,32]{1,0:T(8,128)(2,1)}, u32[]{:S(2)}) copy-start(bf16[128,32]{1,0:T(8,128)(2,1)} %constant.20.clone.lone_t) | copy-start | bytes 24580
  16.5 35.5 %copy-start.1 = (bf16[8192,128]{1,0:T(8,128)(2,1)}, bf16[8192,128]{1,0:T(8,128)(2,1)S(1)}, u32[]{:S(2)}) copy-start(bf16[8192,128]{1,0:T(8,128)(2,1)S(1)} %get-tuple-element.132.weight) | copy-start | bytes 6291460
  16.5 36.1 %copy-start.6 = (f32[1,256,128]{2,1,0:T(8,128)S(1)}, f32[1,256,128]{2,1,0:T(8,128)}, u32[]{:S(2)}) copy-start(f32[1,256,128]{2,1,0:T(8,128)} %param.14) | copy-start | bytes 393220
  16.5 36.1 %copy-start.9 = (s32[1,256,1]{1,2,0:T(1,128)S(1)}, s32[1,256,1]{1,2,0:T(1,128)}, u32[]{:S(2)}) copy-start(s32[1,256,1]{1,2,0:T(1,128)} %param.16) | copy-start | bytes 3076
  16.5 36.1 %copy-start.10 = (s32[1,256]{1,0:T(1,128)S(1)}, s32[1,256]{1,0:T(1,128)}, u32[]{:S(2)}) copy-start(s32[1,256]{1,0:T(1,128)} %cell.1) | copy-start | bytes 3076
  16.6 36.1 %copy-start.11 = (s32[1,256]{1,0:T(1,128)S(1)}, s32[1,256]{1,0:T(1,128)}, u32[]{:S(2)}) copy-start(s32[1,256]{1,0:T(1,128)} %plane.1) | copy-start | bytes 3076

commit v6 on v5

--- a/solution.py
+++ b/solution.py
@@ -171,7 +171,7 @@
             return 0
 
         fetch.wait()
-        lax.fori_loop(0, NW, prepare, 0, unroll=2)
+        lax.fori_loop(0, NW, prepare, 0, unroll=4)
 
     def wait(i, _):
         copy(i).wait()
@@ -425,7 +425,7 @@
         lax.fori_loop(0, 8, pack, part, unroll=8)
         if turn == 0:
             pl.semaphore_wait(barrier, jnp.where(stays, greeted - 1, greeted))
-        lax.fori_loop(0, 8, start, part)
+        lax.fori_loop(0, 8, start, part, unroll=True)
     if first:
         known = jnp.where(iota((NT, 128), 1) < 112, 0, facts[...]).astype(F32)
         known = jnp.max(jnp.max(known, axis=0, keepdims=True), axis=1, keepdims=True)
@@ -459,7 +459,7 @@
         wide[pl.ds(t * WS, 64), :] = block
         return 0
 
-    lax.fori_loop(0, NT, widen, 0, unroll=4)
+    lax.fori_loop(0, NT, widen, 0, unroll=16)
 
     def over_tiles(l, _):
         rows = [wide[pl.ds(2 * l + q, NT, stride=WS), :] for q in range(2)]
@@ -467,7 +467,7 @@
         middle[pl.ds(l * MS, 128), :] = got[:128] + got[128:]
         return 0
 
-    lax.fori_loop(0, 32, over_tiles, 0, unroll=8)
+    lax.fori_loop(0, 32, over_tiles, 0, unroll=32)
     added = dot(lone_t[...], lone[...].reshape(NT, 128).astype(BF))
     wide[0:64, :] = added[:64] - pltpu.roll(added[64:], 96, 1)
 
@@ -520,8 +520,8 @@
         return h
 
     for h in range(2):
-        lax.fori_loop(0, 8, over_columns, h, unroll=4)
-        lax.fori_loop(0, 16, start_b, h)
+        lax.fori_loop(0, 8, over_columns, h, unroll=8)
+        lax.fori_loop(0, 16, start_b, h, unroll=8)
 
     @pl.when(stays)
     def _():

time: 53.7 us -> 52 us (0.968)
  Pallas kernels: 50.6 us -> 48.8 us
    pallas_call x1, Pallas kernels: 28.3 us -> 26.5 us  [finish(): pl.pallas_call(functools.partial(finish_body, first), out_shape=shapes, i...]
where the time goes in v6:
time: 52 us; the launch traced here: 51.8 us
  Pallas kernels  48.8 us (94%)
  local copies, waits for them, and re-layouts  1.89 us (4%)
  between operations  0.85 us (2%)
    pallas_call x1, Pallas kernels, finish(): pl.pallas_call(functools.partial(finish_body, first), out_shape=shapes, i...  26.5 us
    pallas_call x1, Pallas kernels, exchange(): pl.pallas_call(functools.partial(exchange_body, first), out_shape=shapes,...  15.3 us
    pallas_call x1, Pallas kernels, add_blocks(): pl.pallas_call(grid_body, out_shape=jax.ShapeDtypeStruct((512 * GS, 128),...  7.09 us
    unnamed x23, local copies, waits for them, and re-layouts  1.89 us

profile of v6, /device:TPU:1, one launch (start us, length us, event | category | flops | bytes accessed | tf_op | source)
XLA Modules:
  0.0 51.8 jit_solution(8646311305871864520)
XLA Ops:
  0.0 0.0 copy-start
  0.0 1.2 %copy-done = bf16[1,32,2,64,128]{4,3,2,1,0:T(8,128)(2,1)S(1)} copy-done((bf16[1,32,2,64,128]{4,3,2,1,0:T(8,128)(2,1)S(1)}, bf16[1,32,2,64,128]{4,3,2,1,0:T(8,128)(2,1)}, u32[]{:S(2)}) %copy-start) | copy-done | bytes 1048600
  1.2 0.0 copy-start.2
  1.2 0.0 copy-start.3
  1.2 0.0 copy-start.5
  1.2 0.0 copy-start.7
  1.2 0.0 copy-start.8
  1.2 15.3 %exchange.1 = (bf16[1024,128]{1,0:T(8,128)(2,1)S(1)}, s32[32,128]{1,0:T(8,128)S(1)}, f32[4096,128]{1,0:T(8,128)S(1)}, bf16[8192,128]{1,0:T(8,128)(2,1)S(1)}) custom-call(f32[256,128]{1,0:T(8,128)} %bitcast.6, s32[1,256]{1,0:T(1,128)} %bitcast.9, s32[1,256]{1,0:T(1,128)} %cell.1, s32[1,256]{1,0:T(1,128)} %plane.1, bf16[4096,128]{1,0:T(8,128)(2,1)S(1)} %bitcast.5), custom_call_target="tpu_custom_call" | custom-call | tf_op jit(solution)/shard_map/exchange/pallas_call | solution.py:207
  16.5 0.0 copy-start.1
  16.5 0.0 copy-start.6
  16.5 0.0 copy-start.9
  16.5 0.0 copy-start.10
  16.6 0.0 copy-start.11
  16.6 7.1 %add_blocks.2.grid = f32[33280,128]{1,0:T(8,128)S(1)} custom-call(s32[32,128]{1,0:T(8,128)S(1)} %get-tuple-element.129.facts, bf16[1024,128]{1,0:T(8,128)(2,1)S(1)} %get-tuple-element.130.recv, f32[4096,128]{1,0:T(8,128)S(1)} %get-tuple-element.131.table, bf16[8192,128]{1,0:T(8,128)(2,1)S(1)} %get-tuple-element.132.weight), custom_call_target="tpu_custom_call" | custom-call | tf_op jit(solution)/shard_map/add_blocks/pallas_call | solution.py:263
  23.7 0.0 copy-done.2
  23.7 0.0 copy-done.3
  23.7 0.0 copy-done.5
  23.7 0.0 copy-done.7
  23.7 0.0 copy-done.8
  23.7 26.5 %finish.1 = (f32[32,256]{1,0:T(8,128)S(1)}, f32[1,1]{1,0:T(1,128)}) custom-call(f32[33280,128]{1,0:T(8,128)S(1)} %add_blocks.2.grid, s32[32,128]{1,0:T(8,128)S(1)} %get-tuple-element.129.facts, bf16[256,256]{1,0:T(8,128)(2,1)S(1)} %copy-done.5, bf16[4096,128]{1,0:T(8,128)(2,1)S(1)} %copy-done.3, bf16[256,64]{1,0:T(8,128)(2,1)S(1)} %copy-done.7, ...), custom_call_target="tpu_custom_call" | custom-call | tf_op jit(solution)/shard_map/finish/pallas_call | solution.py:604
  50.2 0.0 copy-done.1
  50.9 0.0 copy-done.6
  50.9 0.0 copy-done.9
  50.9 0.0 copy-done.10
  51.0 0.0 copy-done.11
  51.0 0.2 conditional.1
  51.2 0.6 %copy.20 = f32[256,32]{0,1:T(8,128)} copy(f32[256,32]{0,1:T(8,128)S(1)} %bitcast.8) | data formatting | bytes 65536
Async XLA Ops:
  0.0 1.2 %copy-start = (bf16[1,32,2,64,128]{4,3,2,1,0:T(8,128)(2,1)S(1)}, bf16[1,32,2,64,128]{4,3,2,1,0:T(8,128)(2,1)}, u32[]{:S(2)}) copy-start(bf16[1,32,2,64,128]{4,3,2,1,0:T(8,128)(2,1)} %param.15) | copy-start | bytes 3145732
  1.2 22.4 %copy-start.2 = (bf16[2048,256]{1,0:T(8,128)(2,1)S(1)}, bf16[2048,256]{1,0:T(8,128)(2,1)}, u32[]{:S(2)}) copy-start(bf16[2048,256]{1,0:T(8,128)(2,1)} %constant.19.clone.over_j) | copy-start | bytes 3145732
  1.2 22.4 %copy-start.3 = (bf16[4096,128]{1,0:T(8,128)(2,1)S(1)}, bf16[4096,128]{1,0:T(8,128)(2,1)}, u32[]{:S(2)}) copy-start(bf16[4096,128]{1,0:T(8,128)(2,1)} %constant.17.clone.over_x) | copy-start | bytes 3145732
  1.2 22.5 %copy-start.5 = (bf16[256,256]{1,0:T(8,128)(2,1)S(1)}, bf16[256,256]{1,0:T(8,128)(2,1)}, u32[]{:S(2)}) copy-start(bf16[256,256]{1,0:T(8,128)(2,1)} %constant.16.clone.over_r) | copy-start | bytes 393220
  1.2 22.5 %copy-start.7 = (bf16[256,64]{1,0:T(8,128)(2,1)S(1)}, bf16[256,64]{1,0:T(8,128)(2,1)}, u32[]{:S(2)}) copy-start(bf16[256,64]{1,0:T(8,128)(2,1)} %constant.18.clone.over_t) | copy-start | bytes 98308
  1.2 22.5 %copy-start.8 = (bf16[128,32]{1,0:T(8,128)(2,1)S(1)}, bf16[128,32]{1,0:T(8,128)(2,1)}, u32[]{:S(2)}) copy-start(bf16[128,32]{1,0:T(8,128)(2,1)} %constant.20.clone.lone_t) | copy-start | bytes 24580
  16.5 33.7 %copy-start.1 = (bf16[8192,128]{1,0:T(8,128)(2,1)}, bf16[8192,128]{1,0:T(8,128)(2,1)S(1)}, u32[]{:S(2)}) copy-start(bf16[8192,128]{1,0:T(8,128)(2,1)S(1)} %get-tuple-element.132.weight) | copy-start | bytes 6291460
  16.5 34.4 %copy-start.6 = (f32[1,256,128]{2,1,0:T(8,128)S(1)}, f32[1,256,128]{2,1,0:T(8,128)}, u32[]{:S(2)}) copy-start(f32[1,256,128]{2,1,0:T(8,128)} %param.14) | copy-start | bytes 393220
  16.5 34.4 %copy-start.9 = (s32[1,256,1]{1,2,0:T(1,128)S(1)}, s32[1,256,1]{1,2,0:T(1,128)}, u32[]{:S(2)}) copy-start(s32[1,256,1]{1,2,0:T(1,128)} %param.16) | copy-start | bytes 3076
  16.5 34.4 %copy-start.10 = (s32[1,256]{1,0:T(1,128)S(1)}, s32[1,256]{1,0:T(1,128)}, u32[]{:S(2)}) copy-start(s32[1,256]{1,0:T(1,128)} %cell.1) | copy-start | bytes 3076
  16.6 34.4 %copy-start.11 = (s32[1,256]{1,0:T(1,128)S(1)}, s32[1,256]{1,0:T(1,128)}, u32[]{:S(2)}) copy-start(s32[1,256]{1,0:T(1,128)} %plane.1) | copy-start | bytes 3076
